TPU v7x, 256 devices: a whole 4x4x8 slice. The times are simulated.
256 devices in a mesh: ctx: 32 (over x, z), head: 8 (over y, core).
Axes of the slice: x: 4, y: 4, z: 8, core: 2. Of those that a mesh axis runs over, the one named last changes fastest.
Arguments:
- queries: bfloat16 [8192, 2048], P('ctx', 'head'), may hold values from -24 to 24
- key_rows: bfloat16 [8192, 2048], P('ctx', 'head'), may hold values from -24 to 24
- value_rows: bfloat16 [8192, 2048], P('ctx', 'head'), may hold values from -6 to 6
- w_out: bfloat16 [2048, 2048], P('head'), may hold values from -0.125 to 0.125
- out_grad: bfloat16 [8192, 2048], P('ctx', 'head'), may hold values from -6 to 6
- tile_kind: int32 [64, 64], replicated, may hold values from 0 to 2, as said below
Outputs:
- layer_out: bfloat16 [8192, 2048], P('ctx', 'head')
- query_grad: bfloat16 [8192, 2048], P('ctx', 'head')
- key_grad: bfloat16 [8192, 2048], P('ctx', 'head')
- value_grad: bfloat16 [8192, 2048], P('ctx', 'head')
- weight_grad: bfloat16 [2048, 2048], P('head', 'ctx')
Inputs may be any that keep to these rules, and one draw needn't show every extreme that they name: `tile_kind`: entry [b, c] is the kind of the tile of query block b and key block c: 0 the tile is skipped, 1 every query of block b sees every key of block c, 2 query i sees key j only where j % 128 <= i % 128. Every diagonal entry is 2. A key block is needed by an index of ctx where some of that index's 2 query blocks has a nonzero entry for it; from the key blocks of any other index of ctx an index needs at most 1, and in every draw some index needs exactly 1 from every other index.
All inputs are finite; a program needn't handle non-finite values.
Results may differ from a plain program's by a relative error of at most 0.034.
Values may be sent and summed in bfloat16 or wider, within the bound.
A program may use at most 64 MiB of HBM per device.

v0:
```python
import jax
import jax.numpy as jnp
from jax import lax
from jax.sharding import PartitionSpec as P

HD = 128
TILE_TOKENS = 128
KEY_BLOCK_LIMIT = 1
GATHERED_BLOCKS = 4


def slot_table(needed):
    count_blocks = needed.shape[1]
    order_rank = jnp.cumsum(needed.astype(jnp.int32), axis=1) - 1
    slot_ids = jnp.arange(KEY_BLOCK_LIMIT, dtype=jnp.int32)
    slot_hits = needed[:, None, :] & (order_rank[:, None, :] == slot_ids[None, :, None])
    filled = jnp.any(slot_hits, axis=2)
    block_index = jnp.sum(
        jnp.where(slot_hits, jnp.arange(count_blocks, dtype=jnp.int32)[None, None, :], 0), axis=2
    )
    return (slot_hits, filled, block_index)


def on_device(queries, key_rows, value_rows, w_out, out_grad, tile_kind):
    device_list = lax.axis_size("ctx")
    own_index = lax.axis_index("ctx")
    rows = queries.shape[0]
    blocks_own = rows // TILE_TOKENS
    feature_width = queries.shape[1]
    heads = feature_width // HD
    scaling = HD ** (-0.5)
    slot_count = device_list * KEY_BLOCK_LIMIT
    group_sum_total = slot_count // GATHERED_BLOCKS
    q_heads = queries.reshape(rows, heads, HD)
    own_pairs = jnp.concatenate([key_rows, value_rows], axis=1)
    my_rows = lax.dynamic_slice_in_dim(tile_kind, own_index * blocks_own, blocks_own, 0)
    my_cols = lax.dynamic_slice_in_dim(tile_kind, own_index * blocks_own, blocks_own, 1)
    own_kind = lax.dynamic_slice_in_dim(my_rows, own_index * blocks_own, blocks_own, 1)
    peers = jnp.arange(device_list, dtype=jnp.int32)
    others = (peers != own_index)[:, None]
    need_send = (jnp.max(my_cols.reshape(device_list, blocks_own, blocks_own), axis=1) > 0) & others
    need_recv = (jnp.max(my_rows.reshape(blocks_own, device_list, blocks_own), axis=0) > 0) & others
    send_hits, send_filled, send_index = slot_table(need_send)
    recv_hits, recv_filled, recv_index = slot_table(need_recv)
    wanted = (peers[:, None] * blocks_own + recv_index).reshape(-1)
    live = recv_filled.reshape(-1)
    live_int = live.astype(jnp.int32)
    slot_kind = jnp.take(my_rows, wanted, axis=1) * live_int[None, :]
    live_count = jnp.sum(live_int)
    placed_blocks = jnp.where(
        live, jnp.cumsum(live_int) - 1, live_count + jnp.cumsum(1 - live_int) - 1
    )
    ordering = jnp.argsort(placed_blocks)
    group_count = (live_count + GATHERED_BLOCKS - 1) // GATHERED_BLOCKS
    piece = lax.all_gather(own_pairs, "ctx", axis=0, tiled=True)
    length = piece.shape[0]
    piece_blocks = length // TILE_TOKENS
    selector = live[:, None] & (
        wanted[:, None] == jnp.arange(piece_blocks, dtype=jnp.int32)[None, :]
    )
    hit = jnp.any(selector, axis=1)
    chosen = jnp.einsum(
        "sb,brc->src",
        selector.astype(jnp.bfloat16),
        piece.reshape(piece_blocks, TILE_TOKENS, piece.shape[1]),
        preferred_element_type=jnp.float32,
    ).astype(jnp.bfloat16)
    prior_value = jnp.zeros((slot_count, TILE_TOKENS, 2 * feature_width), jnp.bfloat16)
    updated = jnp.where(hit[:, None, None], chosen, prior_value)
    packed = jnp.take(updated, ordering, axis=0).reshape(
        group_sum_total, GATHERED_BLOCKS * TILE_TOKENS, 2 * feature_width
    )
    packed_kind = (
        jnp.take(slot_kind, ordering, axis=1)
        .reshape(blocks_own, group_sum_total, GATHERED_BLOCKS)
        .transpose(1, 0, 2)
    )
    query_pos = jnp.arange(rows, dtype=jnp.int32) % TILE_TOKENS

    def masked_scores(pairs, kinds):
        span = kinds.shape[1]
        key_piece = pairs[:, :feature_width].reshape(span * TILE_TOKENS, heads, HD)
        raw = (
            jnp.einsum("thd,khd->htk", q_heads, key_piece, preferred_element_type=jnp.float32)
            * scaling
        )
        spread = jnp.broadcast_to(
            kinds[:, None, :, None], (blocks_own, TILE_TOKENS, span, TILE_TOKENS)
        ).reshape(rows, span * TILE_TOKENS)
        key_pos = jnp.arange(span * TILE_TOKENS, dtype=jnp.int32) % TILE_TOKENS
        allowed = (spread == 1) | (spread == 2) & (query_pos[:, None] >= key_pos[None, :])
        return jnp.where(allowed[None], raw, -jnp.inf)

    first_scores = masked_scores(own_pairs, own_kind)
    row_max = jnp.max(first_scores, axis=2)
    row_total = jnp.sum(jnp.exp(first_scores - row_max[..., None]), axis=2)

    def stat_step(group, carry):
        run_max, run_total = carry
        scores = masked_scores(packed[group], packed_kind[group])
        new_max = jnp.maximum(run_max, jnp.max(scores, axis=2))
        new_total = run_total * jnp.exp(run_max - new_max) + jnp.sum(
            jnp.exp(scores - new_max[..., None]), axis=2
        )
        return (new_max, new_total)

    row_max, row_total = lax.fori_loop(0, group_count, stat_step, (row_max, row_total))
    log_total = row_max + jnp.log(row_total)

    def value_terms(pairs, kinds):
        scores = masked_scores(pairs, kinds)
        probs = jnp.exp(scores - log_total[..., None]).astype(jnp.bfloat16)
        value_piece = pairs[:, feature_width:].reshape(-1, heads, HD)
        return jnp.einsum("htk,khd->thd", probs, value_piece, preferred_element_type=jnp.float32)

    def value_step(group, total):
        return total + value_terms(packed[group], packed_kind[group])

    attn_sum = lax.fori_loop(0, group_count, value_step, value_terms(own_pairs, own_kind))
    attn = attn_sum.reshape(rows, feature_width).astype(jnp.bfloat16)
    partial_out = jnp.dot(attn, w_out, preferred_element_type=jnp.float32)
    layer_out = lax.psum_scatter(partial_out, "head", scatter_dimension=1, tiled=True).astype(
        jnp.bfloat16
    )
    piece = lax.all_gather(out_grad, "head", axis=1, tiled=True)
    grad_total = jnp.einsum("tc,wc->tw", piece, w_out, preferred_element_type=jnp.float32)
    weight_part = jnp.einsum("tw,tc->wc", attn, piece, preferred_element_type=jnp.float32)
    grad_total, weight_term = (grad_total, weight_part)
    weight_grad = lax.psum_scatter(weight_term, "ctx", scatter_dimension=1, tiled=True).astype(
        jnp.bfloat16
    )
    d_attn = grad_total.astype(jnp.bfloat16)
    grad_heads = d_attn.reshape(rows, heads, HD)
    delta = jnp.sum(
        grad_heads.astype(jnp.float32) * attn.reshape(rows, heads, HD).astype(jnp.float32), axis=2
    ).T

    def grad_terms(pairs, kinds):
        scores = masked_scores(pairs, kinds)
        probs = jnp.exp(scores - log_total[..., None])
        key_piece = pairs[:, :feature_width].reshape(-1, heads, HD)
        value_piece = pairs[:, feature_width:].reshape(-1, heads, HD)
        dprobs = jnp.einsum(
            "thd,khd->htk", grad_heads, value_piece, preferred_element_type=jnp.float32
        )
        dscores = (probs * (dprobs - delta[..., None]) * scaling).astype(jnp.bfloat16)
        query_piece = jnp.einsum(
            "htk,khd->thd", dscores, key_piece, preferred_element_type=jnp.float32
        )
        key_piece_grad = jnp.einsum(
            "htk,thd->khd", dscores, q_heads, preferred_element_type=jnp.float32
        )
        value_piece_grad = jnp.einsum(
            "htk,thd->khd",
            probs.astype(jnp.bfloat16),
            grad_heads,
            preferred_element_type=jnp.float32,
        )
        span_rows = key_piece.shape[0]
        pair_grad = jnp.concatenate(
            [
                key_piece_grad.reshape(span_rows, feature_width),
                value_piece_grad.reshape(span_rows, feature_width),
            ],
            axis=1,
        ).astype(jnp.bfloat16)
        return (query_piece, pair_grad)

    query_total, own_grad = grad_terms(own_pairs, own_kind)

    def grad_step(group, carry):
        query_acc, stored_blocks = carry
        query_piece, pair_grad = grad_terms(packed[group], packed_kind[group])
        return (
            query_acc + query_piece,
            lax.dynamic_update_index_in_dim(stored_blocks, pair_grad, group, 0),
        )

    query_total, stored_blocks = lax.fori_loop(
        0,
        group_count,
        grad_step,
        (
            query_total,
            jnp.zeros(
                (group_sum_total, GATHERED_BLOCKS * TILE_TOKENS, 2 * feature_width), jnp.bfloat16
            ),
        ),
    )
    returned_blocks = jnp.take(
        stored_blocks.reshape(slot_count, TILE_TOKENS, 2 * feature_width), placed_blocks, axis=0
    ).reshape(device_list, KEY_BLOCK_LIMIT, TILE_TOKENS, 2 * feature_width)
    incoming = lax.all_to_all(returned_blocks, "ctx", split_axis=0, concat_axis=0, tiled=True)
    own_grad = lax.optimization_barrier(own_grad)
    summed = own_grad.reshape(blocks_own, TILE_TOKENS, 2 * feature_width).astype(
        jnp.float32
    ) + jnp.einsum(
        "psj,psrc->jrc",
        send_hits.astype(jnp.bfloat16),
        incoming,
        preferred_element_type=jnp.float32,
    )
    key_grad = summed[:, :, :feature_width].reshape(rows, feature_width).astype(jnp.bfloat16)
    value_grad = summed[:, :, feature_width:].reshape(rows, feature_width).astype(jnp.bfloat16)
    query_grad = query_total.reshape(rows, feature_width).astype(jnp.bfloat16)
    return (layer_out, query_grad, key_grad, value_grad, weight_grad)


def solution(mesh):
    in_specs = (
        P("ctx", "head"),
        P("ctx", "head"),
        P("ctx", "head"),
        P("head", None),
        P("ctx", "head"),
        P(),
    )
    out_specs = (
        P("ctx", "head"),
        P("ctx", "head"),
        P("ctx", "head"),
        P("ctx", "head"),
        P("head", "ctx"),
    )
    return jax.shard_map(
        on_device, mesh=mesh, in_specs=in_specs, out_specs=out_specs, check_vma=False
    )
```

profile of v0, /device:TPU:1, one launch (start us, length us, event | category | flops | bytes accessed | tf_op | source)
XLA Modules:
  0.0 478.6 jit_solution(15372056389027196298)
XLA Ops:
  7.2 1.8 pad_maximum_fusion.1
  16.0 1.6 sort.17
  21.3 1.0 copy.173
  22.5 1.1 fusion.93
  23.7 88.6 %all-gather.3.cloned.1.call-done = bf16[8192,512]{1,0:T(8,128)(2,1)} async-done(((bf16[256,512]{1,0:T(8,128)(2,1)}), bf16[8192,512]{1,0:T(8,128)(2,1)}) %all-gather.3.cloned.1.call-update) | async-done | bytes 8388624 | tf_op jit(solution)/shard_map/all_gather | solution.py:55
  112.3 13.4 %convert_select_fusion = bf16[32,128,512]{2,0,1:T(8,128)(2,1)S(1)} fusion(pred[32]{0:T(512)(128)(4,1)S(1)} %fusion.75, bf16[64,128,512]{2,1,0:T(8,128)(2,1)} %bitcast.359, s32[32]{0:T(128)S(1)} %multiply_add_fusion.1, pred[32]{0:T(512)(128)(4,1)S(1)} %reduce_or.18), kind=kOutput, calls=%fused_computation.84 | convolution fusion | flops 272633856 | bytes 12583104 | tf_op jit(solution)/shard_map/sb,brc->src/dot_general | solution.py:62
  125.7 4.5 copy.183
  130.2 5.0 %gather_fusion.2 = bf16[32,128,512]{2,1,0:T(8,128)(2,1)} fusion(bf16[32,128,512]{2,1,0:T(8,128)(2,1)} %copy.183, s32[1024]{0:T(1024)S(1)} %pad_clamp_fusion.1), kind=kCustom, calls=%fused_computation.clone | custom fusion | bytes 8388736 | tf_op jit(solution)/shard_map/jit(_take)/gather | solution.py:70
  135.2 4.7 broadcast_select_fusion
  139.9 6.5 %copy.185 = bf16[8,512,512]{1,2,0:T(8,128)(2,1)} copy(bf16[8,512,512]{2,1,0:T(8,128)(2,1)} %bitcast.333) | data formatting | bytes 8388608
  146.3 5.0 %while.43 = (s32[]{:T(128)}, f32[2,256]{1,0:T(2,128)S(1)}, f32[2,256]{1,0:T(2,128)S(1)}, s32[]{:T(128)}, s32[8,2,4]{2,1,0:T(2,128)S(1)}, /*index=5*/bf16[8,512,5...) while((s32[]{:T(128)}, f32[2,256]{1,0:T(2,128)S(1)}, ...), condition=%wide.region_14.16_spmd.clone, body=%wide.region_11.15_spmd.clone.sunk | while | flops 68818448 | bytes 5144791 | solution.py:107
  147.1 1.1 dynamic-slice_bitcast_fusion.6
  149.6 1.1 dynamic-slice_bitcast_fusion.6
  151.8 5.2 %while.44 = (s32[]{:T(128)}, f32[256,2,128]{0,2,1:T(8,128)S(1)}, s32[]{:T(128)}, bf16[8,512,512]{1,2,0:T(8,128)(2,1)}, s32[8,2,4]{2,1,0:T(2,128)S(1)}, /*index=5...) while((s32[]{:T(128)}, f32[256,2,128]{0,2,1:T(8,128)S(1)}, ...), condition=%wide.region_16.18_spmd.clone, body=%wide.region_15.17_spmd.clone.sunk | while | flops 135729680 | bytes 4333783 | solution.py:119
  152.6 1.1 dynamic-slice_bitcast_fusion.7
  155.2 1.1 dynamic-slice_bitcast_fusion.7
  157.0 1.8 multiply_reduce_fusion
  160.0 1.1 copy.198
  161.1 1.9 fusion.95
  163.0 2.4 broadcast_in_dim.232.clone
  165.4 9.4 %while.45 = (s32[]{:T(128)}, f32[256,2,128]{0,2,1:T(8,128)S(1)}, bf16[8,512,512]{2,1,0:T(8,128)(2,1)}, s32[]{:T(128)}, bf16[8,512,512]{1,2,0:T(8,128)(2,1)}, /*i...) while((s32[]{:T(128)}, f32[256,2,128]{0,2,1:T(8,128)S(1)}, ...), condition=%wide.region_20.22_spmd.clone, body=%wide.region_19.21_spmd.clone.sunk | while | flops 339415552 | bytes 13379827 | solution.py:179
  166.2 1.1 dynamic-slice_bitcast_fusion.8
  170.9 1.1 dynamic-slice_bitcast_fusion.8
  174.8 5.2 %gather_fusion.3 = bf16[32,128,512]{2,1,0:T(8,128)(2,1)} fusion(bf16[32,128,512]{2,1,0:T(8,128)(2,1)} %bitcast.332, s32[1024]{0:T(1024)} %pad_clamp_fusion), kind=kCustom, calls=%fused_computation.1.clone | custom fusion | bytes 8388736 | tf_op jit(solution)/shard_map/jit(_take)/gather | solution.py:190
  179.9 4.7 select_bitcast_fusion
  184.6 64.3 %all-to-all-start = ((bf16[32,1,128,512]{3,2,1,0:T(8,128)(2,1)}), bf16[32,1,128,512]{3,2,1,0:T(8,128)(2,1)}, u32[]{:S(2)}, u32[]{:S(2)}) async-start(bf16[32,1,128,512]{3,2,1,0:T(8,128)(2,1)} %select_bitcast_fusion), calls=%async_computation.1 | async-start | bytes 8388608 | tf_op jit(solution)/shard_map/all_to_all | solution.py:193
  249.2 1.8 fusion.94
  252.6 171.8 %reduce-scatter.5.cloned.1.call-done = f32[256,64]{0,1:T(8,128)} async-done(((f32[256,2048]{0,1:T(8,128)}), f32[256,64]{0,1:T(8,128)}) %reduce-scatter.5.cloned.1.call-update) | async-done | bytes 65552 | tf_op jit(solution)/shard_map/reduce_scatter | solution.py:129
  424.4 1.5 convert_element_type.133
  425.9 38.2 %reduce-scatter.3.cloned.1.call-done = f32[256,256]{1,0:T(8,128)} async-done(((f32[256,2048]{1,0:T(8,128)}), f32[256,256]{1,0:T(8,128)}) %reduce-scatter.3.cloned.1.call-update) | async-done | bytes 262160 | tf_op jit(solution)/shard_map/reduce_scatter | solution.py:122
  464.1 1.6 convert_element_type.121
  465.7 4.8 %fusion.58 = bf16[2,128,512]{2,0,1:T(2,128)(2,1)S(1)} fusion(bf16[32,1,128,512]{3,2,1,0:T(8,128)(2,1)} %all-to-all-done, f32[2,128,512]{2,1,0:T(8,128)S(1)} %convert.31, s32[32,2]{0,1:T(2,128)S(1)} %reduce_window_sum.27, pred[32]{0:T(512)(128)(4,1)S(1)} %copy-done.9, s32[32,2]{0,1:T(2,128)S(1)} %copy-done.5), kind=kOutput, calls=%fused_computation.93 | convolution fusion | flops 8651072 | bytes 4981280 | tf_op jit(solution)/shard_map/psj,psrc->jrc/dot_general | solution.py:197
  (174 shorter events, 27.7 us)
Async XLA Ops:
  7.2 149.8 %copy-start = (bf16[256,2048]{1,0:T(8,128)(2,1)S(1)}, bf16[256,2048]{1,0:T(8,128)(2,1)}, u32[]{:S(2)}) copy-start(bf16[256,2048]{1,0:T(8,128)(2,1)} %param.17) | copy-start | bytes 3145732
  7.2 105.1 %all-gather.3.cloned.1.call-start = ((), (), s32[]{:S(2)}) async-start(), calls=%async_computation.3 | async-start | bytes 8650752 | tf_op jit(solution)/shard_map/all_gather | solution.py:55
  9.0 148.0 %all-gather.5.cloned.1.call-start = ((), (), s32[]{:S(2)}) async-start(), calls=%async_computation.5 | async-start | bytes 1179648 | tf_op jit(solution)/shard_map/all_gather | solution.py:125
  9.8 414.7 %reduce-scatter.5.cloned.1.call-start = ((), (), s32[]{:S(2)}) async-start(), calls=%async_computation.6 | async-start | bytes 2162688 | tf_op jit(solution)/shard_map/reduce_scatter | solution.py:129
  9.8 5.5 %copy-start.8 = (pred[32]{0:T(512)(128)(4,1)}, pred[32]{0:T(512)(128)(4,1)S(1)}, u32[]{:S(2)}) copy-start(pred[32]{0:T(512)(128)(4,1)S(1)} %iota_compare_fusion.1) | copy-start | bytes 100
  11.9 0.6 copy-start.4
  146.3 5.0 %copy-start.2 = (bf16[256,256]{1,0:T(8,128)(2,1)S(1)}, bf16[256,256]{1,0:T(8,128)(2,1)}, u32[]{:S(2)}) copy-start(bf16[256,256]{1,0:T(8,128)(2,1)} %param.16) | copy-start | bytes 393220
  151.8 7.3 %copy-start.3 = (bf16[256,256]{1,0:T(8,128)(2,1)S(1)}, bf16[256,256]{1,0:T(8,128)(2,1)}, u32[]{:S(2)}) copy-start(bf16[256,256]{1,0:T(8,128)(2,1)} %param.15) | copy-start | bytes 393220
  157.0 4.1 copy-start.1
  174.8 5.2 %copy-start.7 = (pred[32]{0:T(512)(128)(4,1)S(1)}, pred[32]{0:T(512)(128)(4,1)}, u32[]{:S(2)}) copy-start(pred[32]{0:T(512)(128)(4,1)} %get-tuple-element.567) | copy-start | bytes 100
  184.6 281.1 %all-to-all-start = ((bf16[32,1,128,512]{3,2,1,0:T(8,128)(2,1)}), bf16[32,1,128,512]{3,2,1,0:T(8,128)(2,1)}, u32[]{:S(2)}, u32[]{:S(2)}) async-start(bf16[32,1,128,512]{3,2,1,0:T(8,128)(2,1)} %select_bitcast_fusion), calls=%async_computation.1 | async-start | bytes 8388608 | tf_op jit(solution)/shard_map/all_to_all | solution.py:193
  248.9 2.1 copy-start.6
  248.9 216.8 %copy-start.5 = (s32[32,2]{0,1:T(2,128)S(1)}, s32[32,2]{0,1:T(2,128)}, u32[]{:S(2)}) copy-start(s32[32,2]{0,1:T(2,128)} %copy-done.4) | copy-start | bytes 772
  248.9 216.8 %copy-start.9 = (pred[32]{0:T(512)(128)(4,1)S(1)}, pred[32]{0:T(512)(128)(4,1)}, u32[]{:S(2)}) copy-start(pred[32]{0:T(512)(128)(4,1)} %copy-done.8) | copy-start | bytes 100
  248.9 215.1 %reduce-scatter.3.cloned.1.call-start = ((), (), s32[]{:S(2)}) async-start(), calls=%async_computation.4 | async-start | bytes 2359296 | tf_op jit(solution)/shard_map/reduce_scatter | solution.py:122
Sparse Core Ops, SparseCore 0:
  10.6 101.6 all-gather.2
  114.1 23.8 all-gather.4
  163.1 261.2 reduce-scatter.4
  427.0 37.0 reduce-scatter.2
where the time goes:
time: 482 us; the launch traced here: 479 us
  waiting for transfers between devices  299 us (62%)
  starting transfers between devices  64.7 us (13%)
  local copies, waits for them, and re-layouts  43.9 us (9%)
  matrix products  32 us (7%)
  other arithmetic  23.4 us (5%)
  between operations  14.8 us (3%)
    reduce_scatter x1, waiting for transfers between devices, on_device(): lax.psum_scatter(weight_term, 'ctx', scatter_dimension=1, tiled=True)  172 us
    all_gather x1, waiting for transfers between devices, on_device(): piece = lax.all_gather(own_pairs, 'ctx', axis=0, tiled=True)  88.6 us
    all_to_all x1, starting transfers between devices, on_device(): lax.all_to_all(returned_blocks, 'ctx', split_axis=0, concat_axis=0, tiled...  64.3 us
    reduce_scatter x1, waiting for transfers between devices, on_device(): lax.psum_scatter(partial_out, 'head', scatter_dimension=1, tiled=True)  38.2 us
    dot_general x1, matrix products, on_device(): jnp.einsum('sb,brc->src', selector.astype(jnp.bfloat16), piece.reshape(pi...  13.4 us
  transfers between devices with their start and end apart: 5, of which 3 were waited for; matrix products, arithmetic and copies ran while one was open for 18% of the time, Pallas kernels for 0%

commit v1 on v0

v1 whole, which is shorter than its diff:
```python
import functools

import jax
import jax.numpy as jnp
from jax import lax
from jax.experimental import pallas as pl
from jax.experimental.pallas import tpu as pltpu
from jax.sharding import PartitionSpec as P

HD = 128
TILE = 128
NX, NY, NZ = 4, 4, 8
TOK = 256
HALF = 512
SCALE = HD ** -0.5
EXP2_SCALE = SCALE * 1.4426950408889634
NEG = -1e30
MESH = pl.DeviceIdType.MESH
BF = jnp.bfloat16
F32 = jnp.float32
NT = (((1,), (1,)), ((), ()))
NN = (((1,), (0,)), ((), ()))
TN = (((0,), (0,)), ((), ()))


def dot(a, b, dims):
    return lax.dot_general(a, b, dims, preferred_element_type=F32)


def kernel(
    q_ref, k_ref, v_ref, w_ref, g_ref, kind_ref,
    out_ref, dq_ref, dk_ref, dv_ref, wg_ref,
    kv, qs, dos, pst, mst, oT, dqT, mrow, lrow, aT, dof,
    g_all, w_all, dsend, gx, osend, afull, aall,
    part, sib_out, sib_in, rs_out, rs_in, wg_out, wg_in, gsend, gin,
    a_send, a_recv, ag_send, ag_recv, sib_send, sib_recv,
    y_send, y_recv, yf_send, yf_recv, w_send, w_recv, d_send, d_recv, gx_send, gx_recv,
    o_send, o_recv, ya_send, ya_recv, yaf_send, yaf_recv,
    rs_send, rs_recv, sb_send, sb_recv, wz_send, wz_recv, f_send, f_recv,
):
    i = lax.axis_index("ctx")
    j = lax.axis_index("head")
    x, z = i // NZ, i % NZ
    y, c = j // 2, j % 2
    xc, xr = x // 2, x % 2

    def dev(x_, z_, y_, c_):
        return (x_ * NZ + z_, y_ * 2 + c_)

    sibling = dev(x, z, y, 1 - c)

    def remote(src, dst, ss, rs, to):
        return pltpu.make_async_remote_copy(
            src_ref=src, dst_ref=dst, send_sem=ss, recv_sem=rs, device_id=to, device_id_type=MESH
        )

    def await_at(dst, sem):
        pltpu.make_async_copy(dst, dst, sem).wait()

    barrier = pltpu.get_barrier_semaphore()
    partners = []
    for dx in range(NX):
        for dc in range(2):
            if dx or dc:
                partners.append(dev((x + dx) % NX, z, y, (c + dc) % 2))
    for dy in range(1, NY):
        for dc in range(2):
            partners.append(dev(x, z, (y + dy) % NY, (c + dc) % 2))
    for dz in range(1, NZ):
        partners.append(dev(x, (z + dz) % NZ, y, c))
    for to in partners:
        pl.semaphore_signal(barrier, inc=1, device_id=to, device_id_type=MESH)
    pl.semaphore_wait(barrier, len(partners))

    my_rows = pl.ds(pl.multiple_of(x * TOK, TOK), TOK)
    q_rows = pl.ds(pl.multiple_of(xr * TOK, TOK), TOK)
    half_rows = pl.ds(pl.multiple_of(c * HALF, HALF), HALF)

    def a_dst(a):
        if a == 2:
            return qs.at[q_rows, :]
        return kv.at[z, a, my_rows, :]

    def a_copies(e, a):
        src = (k_ref, v_ref, q_ref)[a].at[:, pl.ds(e * HD, HD)]
        far = remote(src, a_dst(a), a_send.at[e, a], a_recv.at[xr, a], dev(2 * c + e, z, y, xc))
        near = pltpu.make_async_copy(src, a_dst(a), a_recv.at[xr, a])
        return far, near

    for a in range(3):
        for e in range(2):
            far, near = a_copies(e, a)
            pl.when(x != 2 * c + e)(far.start)
            pl.when(x == 2 * c + e)(near.start)

    def y_copies(k, src, dst, ss, rs):
        if k == 0:
            return remote(src, dst.at[j], ss.at[0], rs.at[0], sibling)
        return remote(src, dst.at[j], ss.at[k], rs.at[k], dev(x, z, (y + k) % NY, c))

    def y_slot(k, core):
        return ((y - k) % NY) * 2 + core

    def y_forward(k, dst, ss, rs):
        slot = y_slot(k, c)
        return remote(dst.at[slot], dst.at[slot], ss.at[k], rs.at[k], sibling)

    for k in (1, 2, 3, 0):
        y_copies(k, g_ref, g_all, y_send, y_recv).start()
    g_all[j] = g_ref[...]
    w_all[j] = w_ref[:, pl.ds(pl.multiple_of(j * TOK, TOK), TOK)]

    def w_copy(k):
        to = (j + k) % 8
        return remote(
            w_ref.at[:, pl.ds(pl.multiple_of(to * TOK, TOK), TOK)], w_all.at[j],
            w_send.at[k], w_recv.at[k], (i, to),
        )

    def w_wait(k):
        await_at(w_all.at[(j - k) % 8], w_recv.at[k])

    def ag_copy(direction, dist, a, zs):
        ref = kv.at[zs, a, half_rows, :]
        step = 1 - 2 * direction
        return remote(
            ref, ref, ag_send.at[direction, dist - 1, a], ag_recv.at[direction, dist - 1, a],
            dev(x, (z + step) % NZ, y, c),
        )

    def sib_copy(t, a, zs):
        ref = kv.at[zs, a, half_rows, :]
        return remote(ref, ref, sib_send.at[t, a], sib_recv.at[t, a], sibling)

    kpos = lax.broadcasted_iota(jnp.int32, (TILE, HALF), 0)
    qpos = lax.broadcasted_iota(jnp.int32, (TILE, HALF), 1) % TILE
    diff = kpos - qpos

    def block_of(half, b, zs):
        return 2 * ((2 * half + b // 2) * NZ + zs) + b % 2

    def forward_unit(zs, half):
        rows = pl.ds(pl.multiple_of(half * HALF, HALF), HALF)
        s = dot(kv[zs, 0, rows, :], qs[...], NT)
        parts = []
        for kb in range(4):
            limits = []
            for qb in range(4):
                kind = kind_ref[block_of(c, qb, z), block_of(half, kb, zs)]
                limit = jnp.where(kind == 1, 1000, jnp.where(kind == 2, 0, -1000))
                limits.append(jnp.full((1, TILE), limit, jnp.int32))
            limit = jnp.concatenate(limits, axis=1)
            parts.append(jnp.where(diff <= limit, s[kb * TILE:(kb + 1) * TILE, :], NEG))
        s = jnp.concatenate(parts, axis=0)
        old = mrow[...]
        new = jnp.maximum(old, jnp.max(s, axis=0, keepdims=True))
        alpha = jnp.exp2((old - new) * EXP2_SCALE)
        p = jnp.exp2((s - new) * EXP2_SCALE)
        lrow[...] = lrow[...] * alpha + jnp.sum(p, axis=0, keepdims=True)
        mrow[...] = new
        mst[zs, half] = new
        pb = p.astype(BF)
        pst[zs, half] = pb
        oT[...] = oT[...] * alpha + dot(kv[zs, 1, rows, :].T, pb, NN)

    mrow[...] = jnp.full(mrow.shape, NEG, F32)
    lrow[...] = jnp.zeros(lrow.shape, F32)
    oT[...] = jnp.zeros(oT.shape, F32)

    def d_copies(e):
        src = dsend.at[:, pl.ds(e * HD, HD)]
        dst = dos.at[q_rows, :]
        far = remote(src, dst, d_send.at[e], d_recv.at[xr], dev(2 * c + e, z, y, xc))
        near = pltpu.make_async_copy(src, dst, d_recv.at[xr])
        return far, near

    def gx_copy(k):
        to = (x + k) % NX
        return remote(
            g_all.at[pl.ds(2 * to, 2)], gx.at[x], gx_send.at[k], gx_recv.at[k], dev(to, z, y, c)
        )

    def forward_step(t, carry):
        dist = (t + 1) // 2
        odd = t % 2
        zs = (z + dist * (1 - 2 * odd)) % NZ

        @pl.when(t == 0)
        def _():
            for a in range(2):
                for r in range(2):
                    await_at(kv.at[z, a, pl.ds(r * TOK, TOK), :], a_recv.at[r, a])
                for direction in range(2):
                    ag_copy(direction, 1, a, z).start()
                sib_copy(t, a, z).start()
            for r in range(2):
                await_at(qs.at[pl.ds(r * TOK, TOK), :], a_recv.at[r, 2])

        @pl.when((odd == 1) & (t < 7))
        def _():
            for a in range(2):
                for direction in range(2):
                    src = (z + dist * (2 * direction - 1)) % NZ
                    await_at(kv.at[src, a, half_rows, :], ag_recv.at[direction, dist - 1, a])
                    forward = ag_copy(direction, dist + 1, a, src)
                    if direction == a:
                        forward.start()
                    else:
                        pl.when(dist < 3)(forward.start)
                    sib_copy(t + direction, a, src).start()

        @pl.when(t == 7)
        def _():
            for a in range(2):
                await_at(kv.at[zs, a, half_rows, :], ag_recv.at[a, 3, a])
                sib_copy(t, a, zs).start()

        @pl.when(t == 4)
        def _():
            for k in (1, 2, 3):
                await_at(g_all.at[y_slot(k, c)], y_recv.at[k])
                y_forward(k, g_all, yf_send, yf_recv).start()

        @pl.when(t == 5)
        def _():
            await_at(g_all.at[y * 2 + 1 - c], y_recv.at[0])
            for k in (1, 2, 3):
                await_at(g_all.at[y_slot(k, 1 - c)], yf_recv.at[k])
            d = jnp.zeros((TOK, TOK), F32)
            for h in range(8):
                d = d + dot(g_all[h], w_ref[:, h * TOK:(h + 1) * TOK], NT)
            dsend[...] = d.astype(BF)
            for e in range(2):
                far, near = d_copies(e)
                pl.when(x != 2 * c + e)(far.start)
                pl.when(x == 2 * c + e)(near.start)
            for k in range(1, NX):
                gx_copy(k).start()
            for h in range(2):
                gx[x, h] = g_all[2 * x + h]
            for k in range(1, 8):
                w_copy(k).start()

        forward_unit(zs, c)
        for a in range(2):
            other = pl.ds(pl.multiple_of((1 - c) * HALF, HALF), HALF)
            await_at(kv.at[zs, a, other, :], sib_recv.at[t, a])
        forward_unit(zs, 1 - c)
        return carry

    lax.fori_loop(0, 8, forward_step, 0)

    inv = 1.0 / lrow[...]
    attnT = (oT[...] * inv).astype(BF).astype(F32)
    aT[...] = attnT
    osend[...] = attnT.T.astype(BF)

    def o_copies(k):
        to = (x + k) % NX
        dst = afull.at[c, :, pl.ds(pl.multiple_of(xr * HD, HD), HD)]
        far = remote(osend, dst, o_send.at[k], o_recv.at[xr, c], dev(to, z, y, xc))
        near = pltpu.make_async_copy(osend, dst, o_recv.at[xr, c])
        return far, near

    for k in range(NX):
        far, near = o_copies(k)
        if k:
            far.start()
        else:
            pl.when(c != xc)(far.start)
            pl.when(c == xc)(near.start)

    for r in range(2):
        await_at(dos.at[pl.ds(r * TOK, TOK), :], d_recv.at[r])
    dof[...] = dos[...].astype(F32).T
    dqT[...] = jnp.zeros(dqT.shape, F32)
    for a in range(2):
        rs_in[a, 3, 1 - a] = jnp.zeros((HALF, HD), BF)

    def sb_copy(u):
        return remote(sib_out.at[u], sib_in.at[u], sb_send.at[u], sb_recv.at[u], sibling)

    def rs_copy(direction, dist, a):
        step = 1 - 2 * direction
        return remote(
            rs_out.at[direction, dist - 1, a], rs_in.at[direction, dist - 1, a],
            rs_send.at[direction, dist - 1, a], rs_recv.at[direction, dist - 1, a],
            dev(x, (z + step) % NZ, y, c),
        )

    def backward_unit(zs, half):
        rows = pl.ds(pl.multiple_of(half * HALF, HALF), HALF)
        factor = jnp.exp2((mst[zs, half] - mrow[...]) * EXP2_SCALE) / lrow[...]
        dob = (dof[...] * factor).astype(BF)
        delta = jnp.sum(dob.astype(F32) * aT[...], axis=0, keepdims=True)
        p = pst[zs, half]
        dv = dot(p, dob, NT)
        dp = dot(kv[zs, 1, rows, :], dob, NN)
        ds = (p.astype(F32) * (dp - delta)).astype(BF)
        dk = dot(ds, qs[...], NN) * SCALE
        dqT[...] += dot(kv[zs, 0, rows, :].T, ds, NN)
        return dk, dv

    def attn_parts_wait():
        for e in range(2):
            for half in range(2):
                await_at(afull.at[half, :, pl.ds(e * HD, HD)], o_recv.at[e, half])

    own_attn = afull.at[xc, q_rows, :]

    def wz_copy(k):
        to = (z + k) % NZ
        return remote(
            wg_out.at[to], wg_in.at[z], wz_send.at[k], wz_recv.at[k], dev(x, to, y, c)
        )

    def backward_step(u, carry):
        dist = (8 - u) // 2
        odd = u % 2
        zs = (z + dist * (2 * odd - 1)) % NZ
        dk, dv = backward_unit(zs, 1 - c)
        sib_out[u, 0] = dk.astype(BF)
        sib_out[u, 1] = dv.astype(BF)
        sb_copy(u).start()
        dk, dv = backward_unit(zs, c)
        part[u, 0] = dk
        part[u, 1] = dv

        def total(v, a):
            return part[v, a] + sib_in[v, a].astype(F32)

        @pl.when(u == 0)
        def _():
            await_at(sib_in.at[u], sb_recv.at[u])
            for a in range(2):
                rs_out[a, 3, a] = total(u, a).astype(BF)
                rs_copy(a, 4, a).start()

        @pl.when((u > 0) & (odd == 0))
        def _():
            for direction in range(2):
                await_at(sib_in.at[u - 1 + direction], sb_recv.at[u - 1 + direction])
            for a in range(2):
                for direction in range(2):
                    incoming = rs_in.at[direction, dist, a]
                    if a == direction:
                        await_at(incoming, rs_recv.at[direction, dist, a])
                    else:
                        @pl.when(dist < 3)
                        def _():
                            await_at(incoming, rs_recv.at[direction, dist, a])
                    value = total(u - 1 + direction, a) + incoming[...].astype(F32)
                    rs_out[direction, dist - 1, a] = value.astype(BF)
                    rs_copy(direction, dist, a).start()

        @pl.when(u == 4)
        def _():
            attn_parts_wait()
            for k in (1, 2, 3, 0):
                y_copies(k, own_attn, aall, ya_send, ya_recv).start()
            aall[j] = own_attn[...]
            for h in range(2):
                wg = jnp.zeros((TOK, TOK), F32)
                for xx in range(NX):
                    if h == 0 and xx > 0:
                        await_at(gx.at[(x - xx) % NX], gx_recv.at[xx])
                for xx in range(NX):
                    at = afull[xx // 2, (xx % 2) * TOK:(xx % 2 + 1) * TOK, :]
                    wg = wg + dot(gx[xx, h], at, TN)
                wg = wg.astype(BF)
                for n in range(4):
                    wg_out[4 * h + n] = wg[n * 64:(n + 1) * 64, :]
            for k in range(1, NZ):
                wz_copy(k).start()
            wg_in[z] = wg_out[z]

        @pl.when(u == 6)
        def _():
            for k in (1, 2, 3):
                await_at(aall.at[y_slot(k, c)], ya_recv.at[k])
                y_forward(k, aall, yaf_send, yaf_recv).start()

        return carry

    lax.fori_loop(0, 8, backward_step, 0)

    def f_copies(r, a):
        src = gsend.at[a, pl.ds(r * TOK, TOK), :]
        dst = gin.at[xr, a]
        far = remote(src, dst, f_send.at[r, a], f_recv.at[xr, a], dev(2 * c + r, z, y, xc))
        near = pltpu.make_async_copy(src, dst, f_recv.at[xr, a])
        return far, near

    def f_start(a):
        for r in range(2):
            far, near = f_copies(r, a)
            pl.when(x != 2 * c + r)(far.start)
            pl.when(x == 2 * c + r)(near.start)

    gsend[0] = (dqT[...] * SCALE).T.astype(BF)
    f_start(0)

    await_at(aall.at[y * 2 + 1 - c], ya_recv.at[0])
    for k in (1, 2, 3):
        await_at(aall.at[y_slot(k, 1 - c)], yaf_recv.at[k])
    for k in range(1, 8):
        w_wait(k)
    o = jnp.zeros((TOK, TOK), F32)
    for h in range(8):
        o = o + dot(aall[h], w_all[h], NN)
    out_ref[...] = o.astype(BF)

    await_at(sib_in.at[7], sb_recv.at[7])
    for a in range(2):
        value = part[7, a] + sib_in[7, a].astype(F32)
        for direction in range(2):
            await_at(rs_in.at[direction, 0, a], rs_recv.at[direction, 0, a])
            value = value + rs_in[direction, 0, a].astype(F32)
        gsend[a + 1] = value.astype(BF)
        f_start(a + 1)

    for k in range(1, NZ):
        await_at(wg_in.at[(z - k) % NZ], wz_recv.at[k])
    wgt = jnp.zeros((64, TOK), F32)
    for n in range(NZ):
        wgt = wgt + wg_in[n].astype(F32)
    wg_ref[...] = wgt.T.astype(BF)

    for a, ref in enumerate((dq_ref, dk_ref, dv_ref)):
        for e in range(2):
            await_at(gin.at[e, a], f_recv.at[e, a])
            ref[:, e * HD:(e + 1) * HD] = gin[e, a]

    for e in range(2):
        for a in range(3):
            far, _ = a_copies(e, a)
            pl.when(x != 2 * c + e)(far.wait_send)
            far, _ = f_copies(e, a)
            pl.when(x != 2 * c + e)(far.wait_send)
        far, _ = d_copies(e)
        pl.when(x != 2 * c + e)(far.wait_send)
    for k in range(NY):
        y_copies(k, g_ref, g_all, y_send, y_recv).wait_send()
        y_copies(k, own_attn, aall, ya_send, ya_recv).wait_send()
        far, _ = o_copies(k)
        if k:
            y_forward(k, g_all, yf_send, yf_recv).wait_send()
            y_forward(k, aall, yaf_send, yaf_recv).wait_send()
            gx_copy(k).wait_send()
            far.wait_send()
        else:
            pl.when(c != xc)(far.wait_send)
    for k in range(1, 8):
        w_copy(k).wait_send()
        wz_copy(k).wait_send()
    for direction in range(2):
        for dist in range(1, 5):
            for a in range(2):
                if dist < 4 or a == direction:
                    ag_copy(direction, dist, a, z).wait_send()
                    rs_copy(direction, dist, a).wait_send()
    for t in range(8):
        sb_copy(t).wait_send()
        for a in range(2):
            sib_copy(t, a, z).wait_send()


def on_device(queries, key_rows, value_rows, w_out, out_grad, tile_kind):
    vmem = pl.BlockSpec(memory_space=pltpu.VMEM)
    smem = pl.BlockSpec(memory_space=pltpu.SMEM)
    V = pltpu.VMEM
    S = lambda *shape: pltpu.SemaphoreType.DMA(shape)
    D = 2048
    scratch = [
        V((NZ, 2, 2 * HALF, HD), BF),
        V((HALF, HD), BF),
        V((HALF, HD), BF),
        V((NZ, 2, HALF, HALF), BF),
        V((NZ, 2, 1, HALF), F32),
        V((HD, HALF), F32),
        V((HD, HALF), F32),
        V((1, HALF), F32),
        V((1, HALF), F32),
        V((HD, HALF), F32),
        V((HD, HALF), F32),
        V((8, TOK, TOK), BF),
        V((8, TOK, TOK), BF),
        V((TOK, TOK), BF),
        V((NX, 2, TOK, TOK), BF),
        V((HALF, HD), BF),
        V((2, HALF, TOK), BF),
        V((8, TOK, TOK), BF),
        V((8, 2, HALF, HD), F32),
        V((8, 2, HALF, HD), BF),
        V((8, 2, HALF, HD), BF),
        V((2, 4, 2, HALF, HD), BF),
        V((2, 4, 2, HALF, HD), BF),
        V((NZ, 64, TOK), BF),
        V((NZ, 64, TOK), BF),
        V((3, HALF, HD), BF),
        V((2, 3, TOK, HD), BF),
        S(2, 3), S(2, 3), S(2, 4, 2), S(2, 4, 2), S(8, 2), S(8, 2),
        S(4), S(4), S(4), S(4), S(8), S(8), S(2), S(2), S(4), S(4),
        S(4), S(2, 2), S(4), S(4), S(4), S(4),
        S(2, 4, 2), S(2, 4, 2), S(8), S(8), S(8), S(8), S(2, 3), S(2, 3),
    ]
    shape = lambda *s: jax.ShapeDtypeStruct(s, BF)
    return pl.pallas_call(
        kernel,
        out_shape=[shape(TOK, TOK)] * 4 + [shape(TOK, 64)],
        in_specs=[vmem] * 5 + [smem],
        out_specs=[vmem] * 5,
        scratch_shapes=scratch,
        compiler_params=pltpu.CompilerParams(
            collective_id=0, has_side_effects=True, vmem_limit_bytes=56 * 1024 * 1024
        ),
        cost_estimate=pl.CostEstimate(flops=8 * 10**9, bytes_accessed=4 * 10**6, transcendentals=0),
    )(queries, key_rows, value_rows, w_out, out_grad, tile_kind)


def solution(mesh):
    in_specs = (
        P("ctx", "head"),
        P("ctx", "head"),
        P("ctx", "head"),
        P("head", None),
        P("ctx", "head"),
        P(),
    )
    out_specs = (
        P("ctx", "head"),
        P("ctx", "head"),
        P("ctx", "head"),
        P("ctx", "head"),
        P("head", "ctx"),
    )
    return jax.shard_map(
        on_device, mesh=mesh, in_specs=in_specs, out_specs=out_specs, check_vma=False
    )
```

time: 482 us -> 89 us (0.18)
  waiting for transfers between devices: 299 us -> 0 us
  Pallas kernels: 0 us -> 81.2 us
  starting transfers between devices: 64.7 us -> 0 us
  local copies, waits for them, and re-layouts: 43.9 us -> 5.7 us
  matrix products: 32 us -> 0 us
  other arithmetic: 23.4 us -> 0 us
  between operations: 14.8 us -> 0.65 us
    reduce_scatter x2 -> x0, waiting for transfers between devices: 210 us -> none  [the longest x1 172 us: on_device(): lax.psum_scatter(weight_term, 'ctx', scatter_dimension=1, tiled=True)]
    all_gather x2 -> x0, waiting for transfers between devices: 88.6 us -> none  [the longest x1 88.6 us: on_device(): piece = lax.all_gather(own_pairs, 'ctx', axis=0, tiled=True)]
    pallas_call x0 -> x1, Pallas kernels: none -> 81.2 us  [on_device(): pl.pallas_call(kernel, out_shape=[shape(TOK, TOK)] * 4 + [shape(TOK, 64)]...]
    all_to_all x1 -> x0, starting transfers between devices: 64.3 us -> none  [on_device(): lax.all_to_all(returned_blocks, 'ctx', split_axis=0, concat_axis=0, tiled...]
    dot_general x25 -> x0, matrix products: 32 us -> none  [the longest x1 13.4 us: on_device(): jnp.einsum('sb,brc->src', selector.astype(jnp.bfloat16), piece.reshape(pi...]
    gather x5 -> x0, local copies, waits for them, and re-layouts: 11.5 us -> none  [the longest x1 5.16 us: on_device(): jnp.take(stored_blocks.reshape(slot_count, TILE_TOKENS, 2 * feature_width...]
    squeeze x6 -> x0, local copies, waits for them, and re-layouts: 6.5 us -> none  [the longest x2 2.17 us: stat_step(): scores = masked_scores(packed[group], packed_kind[group])]
    unnamed x28 -> x10, local copies, waits for them, and re-layouts: 9.03 us -> 4.16 us
  transfers between devices with their start and end apart: 5 -> 0, of which waited for: 3 -> 0; matrix products, arithmetic and copies ran while one was open for 18% -> 0% of each run, Pallas kernels for 0% -> 0%
where the time goes in v1:
time: 89 us; the launch traced here: 87.6 us
  Pallas kernels  81.2 us (91%)
  local copies, waits for them, and re-layouts  5.7 us (6%)
    pallas_call x1, Pallas kernels, on_device(): pl.pallas_call(kernel, out_shape=[shape(TOK, TOK)] * 4 + [shape(TOK, 64)]...  81.2 us
    unnamed x10, local copies, waits for them, and re-layouts  4.16 us

profile of v1, /device:TPU:1, one launch (start us, length us, event | category | flops | bytes accessed | tf_op | source)
XLA Modules:
  0.0 87.6 jit_solution(1108682681719748986)
XLA Ops:
  0.6 81.2 %shard_map.101 = (bf16[256,256]{1,0:T(8,128)(2,1)}, bf16[256,256]{1,0:T(8,128)(2,1)}, bf16[256,256]{1,0:T(8,128)(2,1)}, bf16[256,256]{1,0:T(8,128)(2,1)}, bf16[256,64]{1,0:T(8,128)(2,1)}) custom-call(bf16[256,256]{1,0:T(8,128)(2,1)} %q_ref.1, bf16[256,256]{1,0:T(8,128)(2,1)} %k_ref.1, bf16[256,256]{1,0:T(8,128)(2,1)} %v_ref.1, bf16[256,2048]{1,0:T(8,128)(2,1)} %w_ref.1, ...), custom_call_target="tpu_custom_call" | custom-call | flops 8000000000 | bytes 4000000 | tf_op jit(solution)/shard_map/pallas_call | solution.py:508
  81.9 1.5 %copy.11 = bf16[256,64]{0,1:T(8,128)(2,1)} copy(bf16[256,64]{1,0:T(8,128)(2,1)} %get-tuple-element.9) | data formatting | bytes 65536 | tf_op jit(solution)/shard_map/pallas_call | solution.py:508
  83.4 0.0 copy-start.2
  83.4 1.6 %copy.16 = bf16[256,256]{1,0:T(8,128)(2,1)} copy(bf16[256,256]{1,0:T(8,128)(2,1)} %get-tuple-element.15) | data formatting | bytes 262144
  85.0 0.0 copy-done.2
  85.0 0.0 copy-start.1
  85.0 0.7 copy.17
  85.7 0.3 copy-done.1
  86.0 0.0 copy-start
  86.0 0.7 copy.18
  86.6 0.3 copy-done
  86.9 0.7 copy.19
Async XLA Ops:
  83.4 1.6 %copy-start.2 = (bf16[256,256]{1,0:T(8,128)(2,1)S(1)}, bf16[256,256]{1,0:T(8,128)(2,1)}, u32[]{:S(2)}) copy-start(bf16[256,256]{1,0:T(8,128)(2,1)} %get-tuple-element.16) | copy-start | bytes 393220
  85.0 1.0 %copy-start.1 = (bf16[256,256]{1,0:T(8,128)(2,1)S(1)}, bf16[256,256]{1,0:T(8,128)(2,1)}, u32[]{:S(2)}) copy-start(bf16[256,256]{1,0:T(8,128)(2,1)} %get-tuple-element.17) | copy-start | bytes 393220
  86.0 1.0 %copy-start = (bf16[256,256]{1,0:T(8,128)(2,1)S(1)}, bf16[256,256]{1,0:T(8,128)(2,1)}, u32[]{:S(2)}) copy-start(bf16[256,256]{1,0:T(8,128)(2,1)} %get-tuple-element.18) | copy-start | bytes 393220

commit v2 on v1

v2 whole, which is shorter than its diff:
```python
import functools

import jax
import jax.numpy as jnp
from jax import lax
from jax.experimental import pallas as pl
from jax.experimental.pallas import tpu as pltpu
from jax.sharding import PartitionSpec as P

HD = 128
TILE = 128
NX, NY, NZ = 4, 4, 8
TOK = 256
HALF = 512
SCALE = HD ** -0.5
EXP2_SCALE = SCALE * 1.4426950408889634
NEG = -1e30
MESH = pl.DeviceIdType.MESH
BF = jnp.bfloat16
F32 = jnp.float32
NT = (((1,), (1,)), ((), ()))
NN = (((1,), (0,)), ((), ()))
TN = (((0,), (0,)), ((), ()))


def dot(a, b, dims):
    return lax.dot_general(a, b, dims, preferred_element_type=F32)


def kernel(
    q_ref, k_ref, v_ref, w_ref, g_ref, kind_ref,
    out_ref, dq_ref, dk_ref, dv_ref, wg_ref,
    kv, qs, dos, pst, mst, oT, dqT, mrow, lrow, aT, dof,
    w_in, g_all, w_all, dsend, gx, osend, afull, aall,
    part, sib_out, sib_in, rs_out, rs_in, wgp, wz_out, wz_in, gsend, gq, gkv,
    l_sem, a_send, a_recv, ag_send, ag_recv, sib_send, sib_recv,
    y_send, y_recv, yf_send, yf_recv, w_send, w_recv, d_send, d_recv,
    gx_send, gx_recv, gxf_send, gxf_recv,
    o_send, o_recv, ya_send, ya_recv, yaf_send, yaf_recv,
    rs_send, rs_recv, sb_send, sb_recv, wz_send, wz_recv, f_send, f_recv, g_send, g_recv,
):
    i = lax.axis_index("ctx")
    j = lax.axis_index("head")
    x, z = lax.div(i, NZ), lax.rem(i, NZ)
    y, c = lax.div(j, 2), lax.rem(j, 2)
    xc, xr = lax.div(x, 2), lax.rem(x, 2)

    def dev(x_, z_, y_, c_):
        return (x_ * NZ + z_, y_ * 2 + c_)

    def zplus(n):
        return lax.rem(z + (n + NZ), NZ)

    def xplus(n):
        return lax.rem(x + (n + NX), NX)

    def yplus(n):
        return lax.rem(y + (n + NY), NY)

    sibling = dev(x, z, y, 1 - c)

    def remote(src, dst, ss, rs, to):
        return pltpu.make_async_remote_copy(
            src_ref=src, dst_ref=dst, send_sem=ss, recv_sem=rs, device_id=to, device_id_type=MESH
        )

    def await_at(dst, sem):
        pltpu.make_async_copy(dst, dst, sem).wait()

    w_load = pltpu.make_async_copy(w_ref, w_in, l_sem.at[0])
    g_load = pltpu.make_async_copy(g_ref, g_all.at[j], l_sem.at[1])
    g_load.start()
    w_load.start()

    barrier = pltpu.get_barrier_semaphore()
    partners = []
    for dx in range(NX):
        for dc in range(2):
            if dx or dc:
                partners.append(dev(xplus(dx), z, y, c if dc == 0 else 1 - c))
    for dy in range(1, NY):
        for dc in range(2):
            partners.append(dev(x, z, yplus(dy), c if dc == 0 else 1 - c))
    for dz in (1, -1):
        partners.append(dev(x, zplus(dz), y, c))
        for r in range(2):
            partners.append(dev(2 * c + r, zplus(dz), y, xc))
    for to in partners:
        pl.semaphore_signal(barrier, inc=1, device_id=to, device_id_type=MESH)
    pl.semaphore_wait(barrier, len(partners))

    my_rows = pl.ds(pl.multiple_of(x * TOK, TOK), TOK)
    q_rows = pl.ds(pl.multiple_of(xr * TOK, TOK), TOK)
    half_rows = pl.ds(pl.multiple_of(c * HALF, HALF), HALF)

    def start_either(far, near, at):
        pl.when(x != 2 * c + at)(far.start)
        pl.when(x == 2 * c + at)(near.start)

    def a_copies(e, a):
        src = (k_ref, v_ref, q_ref)[a].at[:, pl.ds(e * HD, HD)]
        dst = qs.at[q_rows, :] if a == 2 else kv.at[z, a, my_rows, :]
        far = remote(src, dst, a_send.at[e, a], a_recv.at[xr, a], dev(2 * c + e, z, y, xc))
        near = pltpu.make_async_copy(src, dst, a_recv.at[xr, a])
        return far, near

    for a in range(3):
        for e in range(2):
            start_either(*a_copies(e, a), e)

    def y_copies(k, src, dst, ss, rs):
        if k == 0:
            return remote(src, dst.at[j], ss.at[0], rs.at[0], sibling)
        return remote(src, dst.at[j], ss.at[k], rs.at[k], dev(x, z, yplus(k), c))

    def y_slot(k, core):
        return yplus(-k) * 2 + core

    def y_forward(k, dst, ss, rs):
        slot = y_slot(k, c)
        return remote(dst.at[slot], dst.at[slot], ss.at[k], rs.at[k], sibling)

    for k in (1, 2, 3, 0):
        y_copies(k, g_ref, g_all, y_send, y_recv).start()

    def w_copy(k):
        to = lax.rem(j + k, 8)
        return remote(
            w_in.at[:, pl.ds(pl.multiple_of(to * TOK, TOK), TOK)], w_all.at[j],
            w_send.at[k], w_recv.at[k], (i, to),
        )

    def w_wait(k):
        await_at(w_all.at[lax.rem(j + 8 - k, 8)], w_recv.at[k])

    def ag_copy(direction, dist, a, zs):
        ref = kv.at[zs, a, half_rows, :]
        return remote(
            ref, ref, ag_send.at[direction, dist - 1, a], ag_recv.at[direction, dist - 1, a],
            dev(x, zplus(1 - 2 * direction), y, c),
        )

    def sib_copy(t, a, zs):
        ref = kv.at[zs, a, half_rows, :]
        return remote(ref, ref, sib_send.at[t, a], sib_recv.at[t, a], sibling)

    kpos = lax.broadcasted_iota(jnp.int32, (TILE, HALF), 0)
    qpos = lax.broadcasted_iota(jnp.int32, (TILE, HALF), 1) % TILE
    diff = kpos - qpos

    def block_of(half, b, zs):
        return 2 * ((2 * half + b // 2) * NZ + zs) + b % 2

    def forward_unit(zs, half):
        rows = pl.ds(pl.multiple_of(half * HALF, HALF), HALF)
        s = dot(kv[zs, 0, rows, :], qs[...], NT)
        parts = []
        for kb in range(4):
            limits = []
            for qb in range(4):
                kind = kind_ref[block_of(c, qb, z), block_of(half, kb, zs)]
                limit = jnp.where(kind == 1, 1000, jnp.where(kind == 2, 0, -1000))
                limits.append(jnp.full((1, TILE), limit, jnp.int32))
            limit = jnp.concatenate(limits, axis=1)
            parts.append(jnp.where(diff <= limit, s[kb * TILE:(kb + 1) * TILE, :], NEG))
        s = jnp.concatenate(parts, axis=0)
        old = mrow[...]
        new = jnp.maximum(old, jnp.max(s, axis=0, keepdims=True))
        alpha = jnp.exp2((old - new) * EXP2_SCALE)
        p = jnp.exp2((s - new) * EXP2_SCALE)
        lrow[...] = lrow[...] * alpha + jnp.sum(p, axis=0, keepdims=True)
        mrow[...] = new
        mst[zs, half] = new
        pb = p.astype(BF)
        pst[zs, half] = pb
        oT[...] = oT[...] * alpha + dot(kv[zs, 1, rows, :].T, pb, NN)

    mrow[...] = jnp.full(mrow.shape, NEG, F32)
    lrow[...] = jnp.zeros(lrow.shape, F32)
    oT[...] = jnp.zeros(oT.shape, F32)
    dqT[...] = jnp.zeros(dqT.shape, F32)
    for a in range(2):
        wz_in[a, 3] = jnp.zeros((64, TOK), BF)

    def d_copies(e):
        src = dsend.at[:, pl.ds(e * HD, HD)]
        dst = dos.at[q_rows, :]
        far = remote(src, dst, d_send.at[e], d_recv.at[xr], dev(2 * c + e, z, y, xc))
        near = pltpu.make_async_copy(src, dst, d_recv.at[xr])
        return far, near

    def gx_copy(k):
        to = xplus(k)
        return remote(
            g_all.at[2 * to + c], gx.at[x, c], gx_send.at[k], gx_recv.at[k], dev(to, z, y, c)
        )

    def gx_forward(k):
        ref = gx.at[xplus(-k), c]
        return remote(ref, ref, gxf_send.at[k], gxf_recv.at[k], sibling)

    def forward_step(t, carry):
        dist = lax.div(t + 1, 2)
        odd = lax.rem(t, 2)
        zs = zplus(dist * (1 - 2 * odd))

        @pl.when(t == 0)
        def _():
            for a in range(2):
                for r in range(2):
                    own = pl.ds(pl.multiple_of(c * HALF, HALF) + r * TOK, TOK)
                    await_at(kv.at[z, a, own, :], a_recv.at[r, a])
                for direction in range(2):
                    ag_copy(direction, 1, a, z).start()
                sib_copy(t, a, z).start()
            for r in range(2):
                await_at(qs.at[pl.ds(r * TOK, TOK), :], a_recv.at[r, 2])

        @pl.when((odd == 1) & (t < 7))
        def _():
            for a in range(2):
                for direction in range(2):
                    src = zplus(dist * (2 * direction - 1))
                    await_at(kv.at[src, a, half_rows, :], ag_recv.at[direction, dist - 1, a])
                    forward = ag_copy(direction, dist + 1, a, src)
                    if direction == a:
                        forward.start()
                    else:
                        pl.when(dist < 3)(forward.start)
                    sib_copy(t + direction, a, src).start()

        @pl.when(t == 7)
        def _():
            for a in range(2):
                await_at(kv.at[zs, a, half_rows, :], ag_recv.at[a, 3, a])
                sib_copy(t, a, zs).start()

        @pl.when(t == 1)
        def _():
            for k in (1, 2, 3):
                await_at(g_all.at[y_slot(k, c)], y_recv.at[k])
                y_forward(k, g_all, yf_send, yf_recv).start()
            g_load.wait()
            w_load.wait()

        @pl.when(t == 2)
        def _():
            await_at(g_all.at[y * 2 + 1 - c], y_recv.at[0])
            for k in (1, 2, 3):
                await_at(g_all.at[y_slot(k, 1 - c)], yf_recv.at[k])
            d = jnp.zeros((TOK, TOK), F32)
            for h in range(8):
                d = d + dot(g_all[h], w_in[:, h * TOK:(h + 1) * TOK], NT)
            dsend[...] = d.astype(BF)
            for e in range(2):
                start_either(*d_copies(e), e)
            for k in range(1, NX):
                gx_copy(k).start()
            for k in range(1, 8):
                w_copy(k).start()
            for h in range(2):
                gx[x, h] = g_all[2 * x + h]
            w_all[j] = w_in[:, pl.ds(pl.multiple_of(j * TOK, TOK), TOK)]

        @pl.when(t == 6)
        def _():
            for r in range(2):
                await_at(dos.at[pl.ds(r * TOK, TOK), :], d_recv.at[r])
            dof[...] = dos[...].astype(F32).T

        forward_unit(zs, c)
        for a in range(2):
            other = pl.ds(pl.multiple_of((1 - c) * HALF, HALF), HALF)
            await_at(kv.at[zs, a, other, :], sib_recv.at[t, a])
        forward_unit(zs, 1 - c)
        return carry

    lax.fori_loop(0, 8, forward_step, 0)

    inv = 1.0 / lrow[...]
    attnT = (oT[...] * inv).astype(BF).astype(F32)
    aT[...] = attnT
    osend[...] = attnT.T.astype(BF)

    def o_copies(k):
        dst = afull.at[c, :, pl.ds(pl.multiple_of(xr * HD, HD), HD)]
        far = remote(osend, dst, o_send.at[k], o_recv.at[xr, c], dev(xplus(k), z, y, xc))
        near = pltpu.make_async_copy(osend, dst, o_recv.at[xr, c])
        return far, near

    for k in range(NX):
        far, near = o_copies(k)
        if k:
            far.start()
        else:
            pl.when(c != xc)(far.start)
            pl.when(c == xc)(near.start)

    def sb_copy(u):
        return remote(sib_out.at[u], sib_in.at[u], sb_send.at[u], sb_recv.at[u], sibling)

    def sb_wait(u):
        await_at(sib_in.at[u], sb_recv.at[u])

    def rs_copy(direction, dist, a):
        return remote(
            rs_out.at[direction, dist - 1, a], rs_in.at[direction, dist - 1, a],
            rs_send.at[direction, dist - 1, a], rs_recv.at[direction, dist - 1, a],
            dev(x, zplus(1 - 2 * direction), y, c),
        )

    def g_copy(direction, r, a):
        return remote(
            rs_out.at[direction, 0, a, pl.ds(r * TOK, TOK), :], gkv.at[direction, xr, a],
            g_send.at[direction, r, a], g_recv.at[direction, xr, a],
            dev(2 * c + r, zplus(1 - 2 * direction), y, xc),
        )

    def total(u, a):
        return part[u, a] + sib_in[u, a].astype(F32)

    def ring(direction, dist, a):
        value = total(0 if dist == 4 else 7 - 2 * dist + direction, a)
        if dist < 3 or (dist == 3 and a == direction):
            await_at(rs_in.at[direction, dist, a], rs_recv.at[direction, dist, a])
            value = value + rs_in[direction, dist, a].astype(F32)
        rs_out[direction, dist - 1, a] = value.astype(BF)
        if dist > 1:
            rs_copy(direction, dist, a).start()
        else:
            for r in range(2):
                g_copy(direction, r, a).start()

    def wz_copy(direction, dist):
        src, dst = wz_out.at[direction, dist - 1], wz_in.at[direction, dist - 1]
        if dist == 4:
            rows = pl.ds(32 * direction, 32)
            src, dst = src.at[rows, :], dst.at[rows, :]
        return remote(
            src, dst, wz_send.at[direction, dist - 1], wz_recv.at[direction, dist - 1],
            dev(x, zplus(1 - 2 * direction), y, c),
        )

    def wz_wait(direction, dist):
        dst = wz_in.at[direction, dist]
        if dist == 3:
            dst = dst.at[pl.ds(32 * direction, 32), :]
        await_at(dst, wz_recv.at[direction, dist])

    def wz_step(dist):
        for direction in range(2):
            value = wgp[zplus(dist * (1 - 2 * direction))]
            if dist < 4:
                wz_wait(direction, dist)
                value = value + wz_in[direction, dist].astype(F32)
            wz_out[direction, dist - 1] = value.astype(BF)
            wz_copy(direction, dist).start()

    def backward_unit(zs, half):
        rows = pl.ds(pl.multiple_of(half * HALF, HALF), HALF)
        factor = jnp.exp2((mst[zs, half] - mrow[...]) * EXP2_SCALE) / lrow[...]
        dob = (dof[...] * factor).astype(BF)
        delta = jnp.sum(dob.astype(F32) * aT[...], axis=0, keepdims=True)
        p = pst[zs, half]
        dv = dot(p, dob, NT)
        dp = dot(kv[zs, 1, rows, :], dob, NN)
        ds = (p.astype(F32) * (dp - delta)).astype(BF)
        dk = dot(ds, qs[...], NN) * SCALE
        dqT[...] += dot(kv[zs, 0, rows, :].T, ds, NN)
        return dk, dv

    own_attn = afull.at[xc, q_rows, :]

    def backward_step(u, carry):
        dist = lax.div(8 - u, 2)
        odd = lax.rem(u, 2)
        zs = zplus(dist * (2 * odd - 1))
        dk, dv = backward_unit(zs, 1 - c)
        sib_out[u, 0] = dk.astype(BF)
        sib_out[u, 1] = dv.astype(BF)
        sb_copy(u).start()
        dk, dv = backward_unit(zs, c)
        part[u, 0] = dk
        part[u, 1] = dv

        @pl.when(u == 0)
        def _():
            sb_wait(0)
            for a in range(2):
                ring(a, 4, a)

        @pl.when(u == 1)
        def _():
            for k in range(1, NX):
                await_at(gx.at[xplus(-k), c], gx_recv.at[k])
                gx_forward(k).start()

        @pl.when(u == 2)
        def _():
            sb_wait(1)
            sb_wait(2)
            for direction in range(2):
                ring(direction, 3, 1 - direction)

        @pl.when(u == 4)
        def _():
            for direction in range(2):
                ring(direction, 3, direction)

        @pl.when(u == 6)
        def _():
            sb_wait(3)
            sb_wait(4)
            for direction in range(2):
                ring(direction, 2, 1 - direction)
            for e in range(2):
                for half in range(2):
                    await_at(afull.at[half, :, pl.ds(e * HD, HD)], o_recv.at[e, half])
            for k in (1, 2, 3, 0):
                y_copies(k, own_attn, aall, ya_send, ya_recv).start()
            for k in range(1, NX):
                await_at(gx.at[xplus(-k), 1 - c], gxf_recv.at[k])
            for h in range(2):
                wg = jnp.zeros((TOK, TOK), F32)
                for xx in range(NX):
                    at = afull[xx // 2, (xx % 2) * TOK:(xx % 2 + 1) * TOK, :]
                    wg = wg + dot(gx[xx, h], at, TN)
                for n in range(4):
                    wgp[4 * h + n] = wg[n * 64:(n + 1) * 64, :]
            wz_step(4)
            aall[j] = own_attn[...]

        return carry

    lax.fori_loop(0, 8, backward_step, 0)

    for direction in range(2):
        ring(direction, 2, direction)

    def f_copies(r, a):
        src = gsend.at[a, pl.ds(r * TOK, TOK), :]
        dst = gkv.at[2, xr, a] if a < 2 else gq.at[xr]
        far = remote(src, dst, f_send.at[r, a], f_recv.at[xr, a], dev(2 * c + r, z, y, xc))
        near = pltpu.make_async_copy(src, dst, f_recv.at[xr, a])
        return far, near

    gsend[2] = (dqT[...] * SCALE).T.astype(BF)
    sb_wait(7)
    for a in range(2):
        gsend[a] = total(7, a).astype(BF)
    for a in range(3):
        for r in range(2):
            start_either(*f_copies(r, a), r)
    wz_step(3)
    sb_wait(5)
    sb_wait(6)
    for direction in range(2):
        ring(direction, 1, 1 - direction)
    wz_step(2)
    for direction in range(2):
        ring(direction, 1, direction)
    for k in (1, 2, 3):
        await_at(aall.at[y_slot(k, c)], ya_recv.at[k])
        y_forward(k, aall, yaf_send, yaf_recv).start()
    wz_step(1)

    for k in range(1, 8):
        w_wait(k)
    await_at(aall.at[y * 2 + 1 - c], ya_recv.at[0])
    for k in (1, 2, 3):
        await_at(aall.at[y_slot(k, 1 - c)], yaf_recv.at[k])
    o = jnp.zeros((TOK, TOK), F32)
    for h in range(8):
        o = o + dot(aall[h], w_all[h], NN)
    out_ref[...] = o.astype(BF)

    for e in range(2):
        for a in range(3):
            far, _ = a_copies(e, a)
            pl.when(x != 2 * c + e)(far.wait_send)
            far, _ = f_copies(e, a)
            pl.when(x != 2 * c + e)(far.wait_send)
        far, _ = d_copies(e)
        pl.when(x != 2 * c + e)(far.wait_send)
    for k in range(NY):
        y_copies(k, g_ref, g_all, y_send, y_recv).wait_send()
        y_copies(k, own_attn, aall, ya_send, ya_recv).wait_send()
        far, _ = o_copies(k)
        if k:
            y_forward(k, g_all, yf_send, yf_recv).wait_send()
            y_forward(k, aall, yaf_send, yaf_recv).wait_send()
            gx_copy(k).wait_send()
            gx_forward(k).wait_send()
            far.wait_send()
        else:
            pl.when(c != xc)(far.wait_send)
    for k in range(1, 8):
        w_copy(k).wait_send()
    for t in range(8):
        sb_copy(t).wait_send()
        for a in range(2):
            sib_copy(t, a, z).wait_send()
    for direction in range(2):
        for dist in range(1, 5):
            for a in range(2):
                if dist < 4 or a == direction:
                    ag_copy(direction, dist, a, z).wait_send()
                    if dist > 1:
                        rs_copy(direction, dist, a).wait_send()

    for e in range(2):
        await_at(gq.at[e], f_recv.at[e, 2])
        dq_ref[:, e * HD:(e + 1) * HD] = gq[e]
    for e in range(2):
        for a in range(2):
            await_at(gkv.at[2, e, a], f_recv.at[e, a])

    for direction in range(2):
        wz_wait(direction, 0)
    wg_ref[...] = (wgp[z] + wz_in[0, 0].astype(F32) + wz_in[1, 0].astype(F32)).astype(BF)
    for direction in range(2):
        for dist in range(1, 5):
            wz_copy(direction, dist).wait_send()

    for a, ref in ((1, dv_ref), (0, dk_ref)):
        for e in range(2):
            for direction in range(2):
                await_at(gkv.at[direction, e, a], g_recv.at[direction, e, a])
            value = gkv[0, e, a].astype(F32) + gkv[1, e, a].astype(F32) + gkv[2, e, a].astype(F32)
            ref[:, e * HD:(e + 1) * HD] = value.astype(BF)
    for direction in range(2):
        for r in range(2):
            for a in range(2):
                g_copy(direction, r, a).wait_send()


def copy_kernel(*refs):
    for n in range(5):
        refs[5 + n][...] = refs[n][...]


def on_device(queries, key_rows, value_rows, w_out, out_grad, tile_kind):
    vmem = pl.BlockSpec(memory_space=pltpu.VMEM)
    smem = pl.BlockSpec(memory_space=pltpu.SMEM)
    anywhere = pl.BlockSpec(memory_space=pl.ANY)
    V = pltpu.VMEM
    S = lambda *shape: pltpu.SemaphoreType.DMA(shape)
    scratch = [
        V((NZ, 2, 2 * HALF, HD), BF),
        V((HALF, HD), BF),
        V((HALF, HD), BF),
        V((NZ, 2, HALF, HALF), BF),
        V((NZ, 2, 1, HALF), F32),
        V((HD, HALF), F32),
        V((HD, HALF), F32),
        V((1, HALF), F32),
        V((1, HALF), F32),
        V((HD, HALF), F32),
        V((HD, HALF), F32),
        V((TOK, 8 * TOK), BF),
        V((8, TOK, TOK), BF),
        V((8, TOK, TOK), BF),
        V((TOK, TOK), BF),
        V((NX, 2, TOK, TOK), BF),
        V((HALF, HD), BF),
        V((2, HALF, TOK), BF),
        V((8, TOK, TOK), BF),
        V((8, 2, HALF, HD), F32),
        V((8, 2, HALF, HD), BF),
        V((8, 2, HALF, HD), BF),
        V((2, 4, 2, HALF, HD), BF),
        V((2, 4, 2, HALF, HD), BF),
        V((NZ, 64, TOK), F32),
        V((2, 4, 64, TOK), BF),
        V((2, 4, 64, TOK), BF),
        V((3, HALF, HD), BF),
        V((2, TOK, HD), BF),
        V((3, 2, 2, TOK, HD), BF),
        S(2), S(2, 3), S(2, 3), S(2, 4, 2), S(2, 4, 2), S(8, 2), S(8, 2),
        S(4), S(4), S(4), S(4), S(8), S(8), S(2), S(2),
        S(4), S(4), S(4), S(4),
        S(4), S(2, 2), S(4), S(4), S(4), S(4),
        S(2, 4, 2), S(2, 4, 2), S(8), S(8), S(2, 4), S(2, 4), S(2, 3), S(2, 3),
        S(2, 2, 2), S(2, 2, 2),
    ]
    shape = lambda *s: jax.ShapeDtypeStruct(s, BF)
    outs = [shape(TOK, TOK)] * 4 + [shape(64, TOK)]
    held = pl.pallas_call(
        kernel,
        out_shape=outs,
        in_specs=[anywhere] * 5 + [smem],
        out_specs=[vmem] * 5,
        scratch_shapes=scratch,
        compiler_params=pltpu.CompilerParams(
            collective_id=0, has_side_effects=True, vmem_limit_bytes=56 * 1024 * 1024
        ),
        cost_estimate=pl.CostEstimate(flops=8 * 10**9, bytes_accessed=4 * 10**6, transcendentals=0),
    )(queries, key_rows, value_rows, w_out, out_grad, tile_kind)
    out, dq, dk, dv, wg = pl.pallas_call(
        copy_kernel, out_shape=outs, in_specs=[vmem] * 5, out_specs=[vmem] * 5
    )(*held)
    return out, dq, dk, dv, wg.T


def solution(mesh):
    in_specs = (
        P("ctx", "head"),
        P("ctx", "head"),
        P("ctx", "head"),
        P("head", None),
        P("ctx", "head"),
        P(),
    )
    out_specs = (
        P("ctx", "head"),
        P("ctx", "head"),
        P("ctx", "head"),
        P("ctx", "head"),
        P("head", "ctx"),
    )
    return jax.shard_map(
        on_device, mesh=mesh, in_specs=in_specs, out_specs=out_specs, check_vma=False
    )
```

time: 89 us -> 78.3 us (0.88); the launches traced: 87.6 us -> 78 us
  local copies, waits for them, and re-layouts: 5.7 us -> 0 us
  Pallas kernels: 81.2 us -> 77.4 us
    unnamed x10 -> x0, local copies, waits for them, and re-layouts: 4.16 us -> none
    pallas_call x1 -> x2, Pallas kernels: 81.2 us -> 77.4 us  [the longest x1 75.5 us: on_device(): pl.pallas_call(kernel, out_shape=outs, in_specs=[anywhere] * 5 + [smem],...]
    pallas_call x1 -> x0, local copies, waits for them, and re-layouts: 1.54 us -> none  [on_device(): pl.pallas_call(kernel, out_shape=[shape(TOK, TOK)] * 4 + [shape(TOK, 64)]...]
where the time goes in v2:
time: 78.3 us; the launch traced here: 78 us
  Pallas kernels  77.4 us (99%)
    pallas_call x1, Pallas kernels, on_device(): pl.pallas_call(kernel, out_shape=outs, in_specs=[anywhere] * 5 + [smem],...  75.5 us
    pallas_call x1, Pallas kernels, on_device(): pl.pallas_call(copy_kernel, out_shape=outs, in_specs=[vmem] * 5, out_spec...  1.9 us

profile of v2, /device:TPU:1, one launch (start us, length us, event | category | flops | bytes accessed | tf_op | source)
XLA Modules:
  0.0 78.0 jit_solution(9150449809226952382)
XLA Ops:
  0.6 75.5 %shard_map.101 = (bf16[256,256]{1,0:T(8,128)(2,1)}, bf16[256,256]{1,0:T(8,128)(2,1)}, bf16[256,256]{1,0:T(8,128)(2,1)}, bf16[256,256]{1,0:T(8,128)(2,1)}, bf16[64,256]{1,0:T(8,128)(2,1)}) custom-call(bf16[256,256]{1,0:T(8,128)(2,1)} %q_ref.1, bf16[256,256]{1,0:T(8,128)(2,1)} %k_ref.1, bf16[256,256]{1,0:T(8,128)(2,1)} %v_ref.1, bf16[256,2048]{1,0:T(8,128)(2,1)} %w_ref.1, ...), custom_call_target="tpu_custom_call" | custom-call | flops 8000000000 | bytes 4000000 | tf_op jit(solution)/shard_map/pallas_call | solution.py:588
  76.1 1.9 %shard_map.102 = (bf16[256,256]{1,0:T(8,128)(2,1)}, bf16[256,256]{1,0:T(8,128)(2,1)}, bf16[256,256]{1,0:T(8,128)(2,1)}, bf16[256,256]{1,0:T(8,128)(2,1)}, bf16[64,256]{1,0:T(8,128)(2,1)}) custom-call(bf16[256,256]{1,0:T(8,128)(2,1)} %get-tuple-element.15.refs_0_, bf16[256,256]{1,0:T(8,128)(2,1)} %get-tuple-element.16.refs_1_, ...), custom_call_target="tpu_custom_call" | custom-call | tf_op jit(solution)/shard_map/pallas_call | solution.py:599

commit v3 on v2

--- a/solution.py
+++ b/solution.py
@@ -74,17 +74,19 @@
 
     barrier = pltpu.get_barrier_semaphore()
     partners = []
-    for dx in range(NX):
-        for dc in range(2):
-            if dx or dc:
-                partners.append(dev(xplus(dx), z, y, c if dc == 0 else 1 - c))
-    for dy in range(1, NY):
-        for dc in range(2):
-            partners.append(dev(x, z, yplus(dy), c if dc == 0 else 1 - c))
+    for dz in (2, -2):
+        partners.append(dev(x, zplus(dz), y, c))
+    for dx in (2, 1, 3):
+        for core in (c, 1 - c):
+            partners.append(dev(xplus(dx), z, y, core))
+    for dy in (2, 1, 3):
+        for core in (c, 1 - c):
+            partners.append(dev(x, z, yplus(dy), core))
     for dz in (1, -1):
-        partners.append(dev(x, zplus(dz), y, c))
         for r in range(2):
             partners.append(dev(2 * c + r, zplus(dz), y, xc))
+        partners.append(dev(x, zplus(dz), y, c))
+    partners.append(sibling)
     for to in partners:
         pl.semaphore_signal(barrier, inc=1, device_id=to, device_id_type=MESH)
     pl.semaphore_wait(barrier, len(partners))
@@ -111,14 +113,14 @@
     def y_copies(k, src, dst, ss, rs):
         if k == 0:
             return remote(src, dst.at[j], ss.at[0], rs.at[0], sibling)
-        return remote(src, dst.at[j], ss.at[k], rs.at[k], dev(x, z, yplus(k), c))
+        return remote(src, dst.at[j], ss.at[0], rs.at[k], dev(x, z, yplus(k), c))
 
     def y_slot(k, core):
         return yplus(-k) * 2 + core
 
     def y_forward(k, dst, ss, rs):
         slot = y_slot(k, c)
-        return remote(dst.at[slot], dst.at[slot], ss.at[k], rs.at[k], sibling)
+        return remote(dst.at[slot], dst.at[slot], ss.at[0], rs.at[k], sibling)
 
     for k in (1, 2, 3, 0):
         y_copies(k, g_ref, g_all, y_send, y_recv).start()
@@ -127,22 +129,25 @@
         to = lax.rem(j + k, 8)
         return remote(
             w_in.at[:, pl.ds(pl.multiple_of(to * TOK, TOK), TOK)], w_all.at[j],
-            w_send.at[k], w_recv.at[k], (i, to),
+            w_send.at[0], w_recv.at[k], (i, to),
         )
 
     def w_wait(k):
         await_at(w_all.at[lax.rem(j + 8 - k, 8)], w_recv.at[k])
 
-    def ag_copy(direction, dist, a, zs):
-        ref = kv.at[zs, a, half_rows, :]
+    def piece(zs, a, r):
+        return kv.at[zs, a, pl.ds(pl.multiple_of(c * HALF + r * TOK, TOK), TOK), :]
+
+    def ag_copy(direction, dist, a, r, zs):
+        ref = piece(zs, a, r)
         return remote(
-            ref, ref, ag_send.at[direction, dist - 1, a], ag_recv.at[direction, dist - 1, a],
+            ref, ref, ag_send.at[direction, dist - 1], ag_recv.at[direction, dist - 1, a, r],
             dev(x, zplus(1 - 2 * direction), y, c),
         )
 
     def sib_copy(t, a, zs):
         ref = kv.at[zs, a, half_rows, :]
-        return remote(ref, ref, sib_send.at[t, a], sib_recv.at[t, a], sibling)
+        return remote(ref, ref, sib_send.at[0], sib_recv.at[t, a], sibling)
 
     kpos = lax.broadcasted_iota(jnp.int32, (TILE, HALF), 0)
     qpos = lax.broadcasted_iota(jnp.int32, (TILE, HALF), 1) % TILE
@@ -180,7 +185,7 @@
     oT[...] = jnp.zeros(oT.shape, F32)
     dqT[...] = jnp.zeros(dqT.shape, F32)
     for a in range(2):
-        wz_in[a, 3] = jnp.zeros((64, TOK), BF)
+        wz_in[1, a] = jnp.zeros((64, TOK), BF)
 
     def d_copies(e):
         src = dsend.at[:, pl.ds(e * HD, HD)]
@@ -192,48 +197,60 @@
     def gx_copy(k):
         to = xplus(k)
         return remote(
-            g_all.at[2 * to + c], gx.at[x, c], gx_send.at[k], gx_recv.at[k], dev(to, z, y, c)
+            g_all.at[2 * to + c], gx.at[x, c], gx_send.at[0], gx_recv.at[k], dev(to, z, y, c)
         )
 
     def gx_forward(k):
         ref = gx.at[xplus(-k), c]
-        return remote(ref, ref, gxf_send.at[k], gxf_recv.at[k], sibling)
+        return remote(ref, ref, gxf_send.at[0], gxf_recv.at[k], sibling)
 
     def forward_step(t, carry):
         dist = lax.div(t + 1, 2)
         odd = lax.rem(t, 2)
         zs = zplus(dist * (1 - 2 * odd))
 
+        def arrival(a, r, dist):
+            for direction in range(2):
+                src = zplus(dist * (2 * direction - 1))
+                await_at(piece(src, a, r), ag_recv.at[direction, dist - 1, a, r])
+                pl.when((dist < 3) | (a == direction))(
+                    ag_copy(direction, dist + 1, a, r, src).start
+                )
+                pl.when(r == 1)(sib_copy(2 * dist - 1 + direction, a, src).start)
+
+        def slot(s):
+            e = s + 1
+
+            @pl.when((s > 2) & (s < 11))
+            def _():
+                arrival(lax.rem(lax.div(e, 2), 2), lax.rem(e, 2), lax.div(e, 4) + 1)
+
         @pl.when(t == 0)
         def _():
             for a in range(2):
                 for r in range(2):
-                    own = pl.ds(pl.multiple_of(c * HALF, HALF) + r * TOK, TOK)
-                    await_at(kv.at[z, a, own, :], a_recv.at[r, a])
-                for direction in range(2):
-                    ag_copy(direction, 1, a, z).start()
+                    await_at(piece(z, a, r), a_recv.at[r, a])
+                    for direction in range(2):
+                        ag_copy(direction, 1, a, r, z).start()
                 sib_copy(t, a, z).start()
             for r in range(2):
                 await_at(qs.at[pl.ds(r * TOK, TOK), :], a_recv.at[r, 2])
 
-        @pl.when((odd == 1) & (t < 7))
+        @pl.when(t == 1)
         def _():
             for a in range(2):
-                for direction in range(2):
-                    src = zplus(dist * (2 * direction - 1))
-                    await_at(kv.at[src, a, half_rows, :], ag_recv.at[direction, dist - 1, a])
-                    forward = ag_copy(direction, dist + 1, a, src)
-                    if direction == a:
-                        forward.start()
-                    else:
-                        pl.when(dist < 3)(forward.start)
-                    sib_copy(t + direction, a, src).start()
+                for r in range(2):
+                    arrival(jnp.int32(a), jnp.int32(r), jnp.int32(1))
 
         @pl.when(t == 7)
         def _():
+            for r in range(2):
+                for a in range(2):
+                    await_at(piece(zs, a, r), ag_recv.at[a, 3, a, r])
             for a in range(2):
-                await_at(kv.at[zs, a, half_rows, :], ag_recv.at[a, 3, a])
                 sib_copy(t, a, zs).start()
+
+        slot(2 * t)
 
         @pl.when(t == 1)
         def _():
@@ -256,6 +273,9 @@
                 start_either(*d_copies(e), e)
             for k in range(1, NX):
                 gx_copy(k).start()
+
+        @pl.when(t == 3)
+        def _():
             for k in range(1, 8):
                 w_copy(k).start()
             for h in range(2):
@@ -269,6 +289,7 @@
             dof[...] = dos[...].astype(F32).T
 
         forward_unit(zs, c)
+        slot(2 * t + 1)
         for a in range(2):
             other = pl.ds(pl.multiple_of((1 - c) * HALF, HALF), HALF)
             await_at(kv.at[zs, a, other, :], sib_recv.at[t, a])
@@ -297,7 +318,7 @@
             pl.when(c == xc)(near.start)
 
     def sb_copy(u):
-        return remote(sib_out.at[u], sib_in.at[u], sb_send.at[u], sb_recv.at[u], sibling)
+        return remote(sib_out.at[u], sib_in.at[u], sb_send.at[0], sb_recv.at[u], sibling)
 
     def sb_wait(u):
         await_at(sib_in.at[u], sb_recv.at[u])
@@ -305,7 +326,7 @@
     def rs_copy(direction, dist, a):
         return remote(
             rs_out.at[direction, dist - 1, a], rs_in.at[direction, dist - 1, a],
-            rs_send.at[direction, dist - 1, a], rs_recv.at[direction, dist - 1, a],
+            rs_send.at[0 if dist == 4 else 1], rs_recv.at[direction, dist - 1, a],
             dev(x, zplus(1 - 2 * direction), y, c),
         )
 
@@ -331,30 +352,38 @@
             for r in range(2):
                 g_copy(direction, r, a).start()
 
-    def wz_copy(direction, dist):
-        src, dst = wz_out.at[direction, dist - 1], wz_in.at[direction, dist - 1]
-        if dist == 4:
+    def wz_copy(kind, direction):
+        src, dst = wz_out.at[kind, direction], wz_in.at[kind, direction]
+        if kind == 1:
             rows = pl.ds(32 * direction, 32)
             src, dst = src.at[rows, :], dst.at[rows, :]
+        far = (1, 2, 1, 2)[kind] * (1 - 2 * direction)
         return remote(
-            src, dst, wz_send.at[direction, dist - 1], wz_recv.at[direction, dist - 1],
-            dev(x, zplus(1 - 2 * direction), y, c),
+            src, dst, wz_send.at[0 if kind == 1 else 1], wz_recv.at[kind, direction],
+            dev(x, zplus(far), y, c),
         )
 
-    def wz_wait(direction, dist):
-        dst = wz_in.at[direction, dist]
-        if dist == 3:
+    def wz_wait(kind, direction):
+        dst = wz_in.at[kind, direction]
+        if kind == 1:
             dst = dst.at[pl.ds(32 * direction, 32), :]
-        await_at(dst, wz_recv.at[direction, dist])
-
-    def wz_step(dist):
+        await_at(dst, wz_recv.at[kind, direction])
+
+    def wz_start():
+        for kind in (1, 0, 2):
+            for direction in range(2):
+                to = zplus((3, 4, 1)[kind] * (1 - 2 * direction))
+                wz_out[kind, direction] = wgp[to].astype(BF)
+                wz_copy(kind, direction).start()
+
+    def wz_middle():
         for direction in range(2):
-            value = wgp[zplus(dist * (1 - 2 * direction))]
-            if dist < 4:
-                wz_wait(direction, dist)
-                value = value + wz_in[direction, dist].astype(F32)
-            wz_out[direction, dist - 1] = value.astype(BF)
-            wz_copy(direction, dist).start()
+            for kind in (1, 0):
+                wz_wait(kind, direction)
+            value = wgp[zplus(2 - 4 * direction)]
+            value = value + wz_in[0, direction].astype(F32) + wz_in[1, direction].astype(F32)
+            wz_out[3, direction] = value.astype(BF)
+            wz_copy(3, direction).start()
 
     def backward_unit(zs, half):
         rows = pl.ds(pl.multiple_of(half * HALF, HALF), HALF)
@@ -371,7 +400,15 @@
 
     own_attn = afull.at[xc, q_rows, :]
 
-    def backward_step(u, carry):
+    def f_copies(r, a):
+        src = gsend.at[a, pl.ds(r * TOK, TOK), :]
+        dst = gkv.at[2, xr, a] if a < 2 else gq.at[xr]
+        far = remote(src, dst, f_send.at[r, a], f_recv.at[xr, a], dev(2 * c + r, z, y, xc))
+        near = pltpu.make_async_copy(src, dst, f_recv.at[xr, a])
+        return far, near
+
+    def backward_step(n, carry):
+        u = jnp.where(n == 5, 7, jnp.where(n > 5, n - 1, n))
         dist = lax.div(8 - u, 2)
         odd = lax.rem(u, 2)
         zs = zplus(dist * (2 * odd - 1))
@@ -402,17 +439,22 @@
             for direction in range(2):
                 ring(direction, 3, 1 - direction)
 
-        @pl.when(u == 4)
+        @pl.when(u == 3)
         def _():
             for direction in range(2):
                 ring(direction, 3, direction)
 
-        @pl.when(u == 6)
+        @pl.when(u == 7)
         def _():
             sb_wait(3)
             sb_wait(4)
             for direction in range(2):
                 ring(direction, 2, 1 - direction)
+            sb_wait(7)
+            for a in range(2):
+                gsend[a] = total(7, a).astype(BF)
+                for r in range(2):
+                    start_either(*f_copies(r, a), r)
             for e in range(2):
                 for half in range(2):
                     await_at(afull.at[half, :, pl.ds(e * HD, HD)], o_recv.at[e, half])
@@ -427,42 +469,31 @@
                     wg = wg + dot(gx[xx, h], at, TN)
                 for n in range(4):
                     wgp[4 * h + n] = wg[n * 64:(n + 1) * 64, :]
-            wz_step(4)
+            wz_start()
             aall[j] = own_attn[...]
 
+        @pl.when(u == 5)
+        def _():
+            for direction in range(2):
+                ring(direction, 2, direction)
+
         return carry
 
     lax.fori_loop(0, 8, backward_step, 0)
 
-    for direction in range(2):
-        ring(direction, 2, direction)
-
-    def f_copies(r, a):
-        src = gsend.at[a, pl.ds(r * TOK, TOK), :]
-        dst = gkv.at[2, xr, a] if a < 2 else gq.at[xr]
-        far = remote(src, dst, f_send.at[r, a], f_recv.at[xr, a], dev(2 * c + r, z, y, xc))
-        near = pltpu.make_async_copy(src, dst, f_recv.at[xr, a])
-        return far, near
-
     gsend[2] = (dqT[...] * SCALE).T.astype(BF)
-    sb_wait(7)
-    for a in range(2):
-        gsend[a] = total(7, a).astype(BF)
-    for a in range(3):
-        for r in range(2):
-            start_either(*f_copies(r, a), r)
-    wz_step(3)
+    for r in range(2):
+        start_either(*f_copies(r, 2), r)
     sb_wait(5)
     sb_wait(6)
     for direction in range(2):
         ring(direction, 1, 1 - direction)
-    wz_step(2)
+    wz_middle()
     for direction in range(2):
         ring(direction, 1, direction)
     for k in (1, 2, 3):
         await_at(aall.at[y_slot(k, c)], ya_recv.at[k])
         y_forward(k, aall, yaf_send, yaf_recv).start()
-    wz_step(1)
 
     for k in range(1, 8):
         w_wait(k)
@@ -482,31 +513,28 @@
             pl.when(x != 2 * c + e)(far.wait_send)
         far, _ = d_copies(e)
         pl.when(x != 2 * c + e)(far.wait_send)
-    for k in range(NY):
-        y_copies(k, g_ref, g_all, y_send, y_recv).wait_send()
-        y_copies(k, own_attn, aall, ya_send, ya_recv).wait_send()
+    far, _ = o_copies(0)
+    pl.when(c != xc)(far.wait_send)
+    for k in range(1, NX):
         far, _ = o_copies(k)
-        if k:
-            y_forward(k, g_all, yf_send, yf_recv).wait_send()
-            y_forward(k, aall, yaf_send, yaf_recv).wait_send()
-            gx_copy(k).wait_send()
-            gx_forward(k).wait_send()
-            far.wait_send()
-        else:
-            pl.when(c != xc)(far.wait_send)
-    for k in range(1, 8):
-        w_copy(k).wait_send()
-    for t in range(8):
-        sb_copy(t).wait_send()
-        for a in range(2):
-            sib_copy(t, a, z).wait_send()
+        far.wait_send()
+
+    def left(ref, sem):
+        remote(ref, ref, sem, sem, sibling).wait_send()
+
+    left(g_all.at[pl.ds(0, 4)], y_send.at[0])
+    left(g_all.at[pl.ds(0, 4)], ya_send.at[0])
+    for sem in (yf_send, yaf_send, gx_send, gxf_send):
+        left(g_all.at[pl.ds(0, 3)], sem.at[0])
+    left(w_all.at[pl.ds(0, 7)], w_send.at[0])
+    left(sib_out, sb_send.at[0])
+    left(kv.at[:, :, pl.ds(0, HALF), :], sib_send.at[0])
+    left(rs_out.at[0, 3], rs_send.at[0])
+    left(rs_out.at[:, pl.ds(1, 2)], rs_send.at[1])
     for direction in range(2):
-        for dist in range(1, 5):
-            for a in range(2):
-                if dist < 4 or a == direction:
-                    ag_copy(direction, dist, a, z).wait_send()
-                    if dist > 1:
-                        rs_copy(direction, dist, a).wait_send()
+        for dist in range(1, 4):
+            left(kv.at[0, :, pl.ds(0, HALF), :], ag_send.at[direction, dist - 1])
+        left(kv.at[0, 0, pl.ds(0, HALF), :], ag_send.at[direction, 3])
 
     for e in range(2):
         await_at(gq.at[e], f_recv.at[e, 2])
@@ -515,12 +543,14 @@
         for a in range(2):
             await_at(gkv.at[2, e, a], f_recv.at[e, a])
 
-    for direction in range(2):
-        wz_wait(direction, 0)
-    wg_ref[...] = (wgp[z] + wz_in[0, 0].astype(F32) + wz_in[1, 0].astype(F32)).astype(BF)
-    for direction in range(2):
-        for dist in range(1, 5):
-            wz_copy(direction, dist).wait_send()
+    wg = wgp[z]
+    for kind in (2, 3):
+        for direction in range(2):
+            wz_wait(kind, direction)
+            wg = wg + wz_in[kind, direction].astype(F32)
+    wg_ref[...] = wg.astype(BF)
+    left(wz_out.at[0, 0], wz_send.at[0])
+    left(wz_out.at[pl.ds(0, 3)], wz_send.at[1])
 
     for a, ref in ((1, dv_ref), (0, dk_ref)):
         for e in range(2):
@@ -571,16 +601,16 @@
         V((2, 4, 2, HALF, HD), BF),
         V((2, 4, 2, HALF, HD), BF),
         V((NZ, 64, TOK), F32),
-        V((2, 4, 64, TOK), BF),
-        V((2, 4, 64, TOK), BF),
+        V((4, 2, 64, TOK), BF),
+        V((4, 2, 64, TOK), BF),
         V((3, HALF, HD), BF),
         V((2, TOK, HD), BF),
         V((3, 2, 2, TOK, HD), BF),
-        S(2), S(2, 3), S(2, 3), S(2, 4, 2), S(2, 4, 2), S(8, 2), S(8, 2),
-        S(4), S(4), S(4), S(4), S(8), S(8), S(2), S(2),
-        S(4), S(4), S(4), S(4),
-        S(4), S(2, 2), S(4), S(4), S(4), S(4),
-        S(2, 4, 2), S(2, 4, 2), S(8), S(8), S(2, 4), S(2, 4), S(2, 3), S(2, 3),
+        S(2), S(2, 3), S(2, 3), S(2, 4), S(2, 4, 2, 2), S(1), S(8, 2),
+        S(1), S(4), S(1), S(4), S(1), S(8), S(2), S(2),
+        S(1), S(4), S(1), S(4),
+        S(4), S(2, 2), S(1), S(4), S(1), S(4),
+        S(2), S(2, 4, 2), S(1), S(8), S(2), S(4, 2), S(2, 3), S(2, 3),
         S(2, 2, 2), S(2, 2, 2),
     ]
     shape = lambda *s: jax.ShapeDtypeStruct(s, BF)

time: 78.3 us -> 74.1 us (0.946)
  Pallas kernels: 77.4 us -> 73.2 us
    pallas_call x1, Pallas kernels: 75.5 us -> 71.3 us  [on_device(): pl.pallas_call(kernel, out_shape=outs, in_specs=[anywhere] * 5 + [smem],...]
where the time goes in v3:
time: 74.1 us; the launch traced here: 73.8 us
  Pallas kernels  73.2 us (99%)
    pallas_call x1, Pallas kernels, on_device(): pl.pallas_call(kernel, out_shape=outs, in_specs=[anywhere] * 5 + [smem],...  71.3 us
    pallas_call x1, Pallas kernels, on_device(): pl.pallas_call(copy_kernel, out_shape=outs, in_specs=[vmem] * 5, out_spec...  1.9 us

profile of v3, /device:TPU:1, one launch (start us, length us, event | category | flops | bytes accessed | tf_op | source)
XLA Modules:
  0.0 73.8 jit_solution(4115530858996313845)
XLA Ops:
  0.6 71.3 %shard_map.101 = (bf16[256,256]{1,0:T(8,128)(2,1)}, bf16[256,256]{1,0:T(8,128)(2,1)}, bf16[256,256]{1,0:T(8,128)(2,1)}, bf16[256,256]{1,0:T(8,128)(2,1)}, bf16[64,256]{1,0:T(8,128)(2,1)}) custom-call(bf16[256,256]{1,0:T(8,128)(2,1)} %q_ref.1, bf16[256,256]{1,0:T(8,128)(2,1)} %k_ref.1, bf16[256,256]{1,0:T(8,128)(2,1)} %v_ref.1, bf16[256,2048]{1,0:T(8,128)(2,1)} %w_ref.1, ...), custom_call_target="tpu_custom_call" | custom-call | flops 8000000000 | bytes 4000000 | tf_op jit(solution)/shard_map/pallas_call | solution.py:618
  71.9 1.9 %shard_map.102 = (bf16[256,256]{1,0:T(8,128)(2,1)}, bf16[256,256]{1,0:T(8,128)(2,1)}, bf16[256,256]{1,0:T(8,128)(2,1)}, bf16[256,256]{1,0:T(8,128)(2,1)}, bf16[64,256]{1,0:T(8,128)(2,1)}) custom-call(bf16[256,256]{1,0:T(8,128)(2,1)} %get-tuple-element.15.refs_0_, bf16[256,256]{1,0:T(8,128)(2,1)} %get-tuple-element.16.refs_1_, ...), custom_call_target="tpu_custom_call" | custom-call | tf_op jit(solution)/shard_map/pallas_call | solution.py:629

commit v4 on v3

--- a/solution.py
+++ b/solution.py
@@ -29,10 +29,10 @@
 
 def kernel(
     q_ref, k_ref, v_ref, w_ref, g_ref, kind_ref,
-    out_ref, dq_ref, dk_ref, dv_ref, wg_ref,
+    out_ref, gq, gkv, wg_ref,
     kv, qs, dos, pst, mst, oT, dqT, mrow, lrow, aT, dof,
     w_in, g_all, w_all, dsend, gx, osend, afull, aall,
-    part, sib_out, sib_in, rs_out, rs_in, wgp, wz_out, wz_in, gsend, gq, gkv,
+    part, sib_out, sib_in, rs_out, rs_in, wgp, wz_out, wz_in, gsend, out_vm, wg_vm,
     l_sem, a_send, a_recv, ag_send, ag_recv, sib_send, sib_recv,
     y_send, y_recv, yf_send, yf_recv, w_send, w_recv, d_send, d_recv,
     gx_send, gx_recv, gxf_send, gxf_recv,
@@ -74,17 +74,12 @@
 
     barrier = pltpu.get_barrier_semaphore()
     partners = []
-    for dz in (2, -2):
-        partners.append(dev(x, zplus(dz), y, c))
     for dx in (2, 1, 3):
         for core in (c, 1 - c):
             partners.append(dev(xplus(dx), z, y, core))
     for dy in (2, 1, 3):
-        for core in (c, 1 - c):
-            partners.append(dev(x, z, yplus(dy), core))
+        partners.append(dev(x, z, yplus(dy), c))
     for dz in (1, -1):
-        for r in range(2):
-            partners.append(dev(2 * c + r, zplus(dz), y, xc))
         partners.append(dev(x, zplus(dz), y, c))
     partners.append(sibling)
     for to in partners:
@@ -145,9 +140,12 @@
             dev(x, zplus(1 - 2 * direction), y, c),
         )
 
-    def sib_copy(t, a, zs):
-        ref = kv.at[zs, a, half_rows, :]
-        return remote(ref, ref, sib_send.at[0], sib_recv.at[t, a], sibling)
+    def pair(zs, core, r):
+        return kv.at[zs, :, pl.ds(pl.multiple_of(core * HALF + r * TOK, TOK), TOK), :]
+
+    def sib_copy(t, r, zs):
+        ref = pair(zs, c, r)
+        return remote(ref, ref, sib_send.at[0], sib_recv.at[t, r], sibling)
 
     kpos = lax.broadcasted_iota(jnp.int32, (TILE, HALF), 0)
     qpos = lax.broadcasted_iota(jnp.int32, (TILE, HALF), 1) % TILE
@@ -209,46 +207,47 @@
         odd = lax.rem(t, 2)
         zs = zplus(dist * (1 - 2 * odd))
 
-        def arrival(a, r, dist):
+        def arrival(e, dist):
+            a, h = lax.rem(e, 2), lax.div(e, 2)
             for direction in range(2):
+                r = h if direction == 0 else 1 - h
                 src = zplus(dist * (2 * direction - 1))
                 await_at(piece(src, a, r), ag_recv.at[direction, dist - 1, a, r])
-                pl.when((dist < 3) | (a == direction))(
-                    ag_copy(direction, dist + 1, a, r, src).start
-                )
-                pl.when(r == 1)(sib_copy(2 * dist - 1 + direction, a, src).start)
+                pl.when((dist < 3) | (h == 0))(ag_copy(direction, dist + 1, a, r, src).start)
+                pl.when(a == 1)(sib_copy(2 * dist - 1 + direction, r, src).start)
 
         def slot(s):
             e = s + 1
 
             @pl.when((s > 2) & (s < 11))
             def _():
-                arrival(lax.rem(lax.div(e, 2), 2), lax.rem(e, 2), lax.div(e, 4) + 1)
+                arrival(lax.rem(e, 4), lax.div(e, 4) + 1)
 
         @pl.when(t == 0)
         def _():
             for a in range(2):
                 for r in range(2):
                     await_at(piece(z, a, r), a_recv.at[r, a])
-                    for direction in range(2):
-                        ag_copy(direction, 1, a, r, z).start()
-                sib_copy(t, a, z).start()
+                    ag_copy(r, 1, a, r, z).start()
+            for r in range(2):
+                sib_copy(t, r, z).start()
+            for a in range(2):
+                for direction in range(2):
+                    ag_copy(direction, 1, a, 1 - direction, z).start()
             for r in range(2):
                 await_at(qs.at[pl.ds(r * TOK, TOK), :], a_recv.at[r, 2])
 
         @pl.when(t == 1)
         def _():
-            for a in range(2):
-                for r in range(2):
-                    arrival(jnp.int32(a), jnp.int32(r), jnp.int32(1))
+            for e in range(4):
+                arrival(jnp.int32(e), jnp.int32(1))
 
         @pl.when(t == 7)
         def _():
             for r in range(2):
                 for a in range(2):
-                    await_at(piece(zs, a, r), ag_recv.at[a, 3, a, r])
-            for a in range(2):
-                sib_copy(t, a, zs).start()
+                    await_at(piece(zs, a, r), ag_recv.at[r, 3, a, r])
+                sib_copy(t, r, zs).start()
 
         slot(2 * t)
 
@@ -290,9 +289,8 @@
 
         forward_unit(zs, c)
         slot(2 * t + 1)
-        for a in range(2):
-            other = pl.ds(pl.multiple_of((1 - c) * HALF, HALF), HALF)
-            await_at(kv.at[zs, a, other, :], sib_recv.at[t, a])
+        for r in range(2):
+            await_at(pair(zs, 1 - c, r), sib_recv.at[t, r])
         forward_unit(zs, 1 - c)
         return carry
 
@@ -301,21 +299,12 @@
     inv = 1.0 / lrow[...]
     attnT = (oT[...] * inv).astype(BF).astype(F32)
     aT[...] = attnT
-    osend[...] = attnT.T.astype(BF)
 
     def o_copies(k):
         dst = afull.at[c, :, pl.ds(pl.multiple_of(xr * HD, HD), HD)]
         far = remote(osend, dst, o_send.at[k], o_recv.at[xr, c], dev(xplus(k), z, y, xc))
         near = pltpu.make_async_copy(osend, dst, o_recv.at[xr, c])
         return far, near
-
-    for k in range(NX):
-        far, near = o_copies(k)
-        if k:
-            far.start()
-        else:
-            pl.when(c != xc)(far.start)
-            pl.when(c == xc)(near.start)
 
     def sb_copy(u):
         return remote(sib_out.at[u], sib_in.at[u], sb_send.at[0], sb_recv.at[u], sibling)
@@ -387,16 +376,26 @@
 
     def backward_unit(zs, half):
         rows = pl.ds(pl.multiple_of(half * HALF, HALF), HALF)
-        factor = jnp.exp2((mst[zs, half] - mrow[...]) * EXP2_SCALE) / lrow[...]
-        dob = (dof[...] * factor).astype(BF)
-        delta = jnp.sum(dob.astype(F32) * aT[...], axis=0, keepdims=True)
-        p = pst[zs, half]
-        dv = dot(p, dob, NT)
-        dp = dot(kv[zs, 1, rows, :], dob, NN)
-        ds = (p.astype(F32) * (dp - delta)).astype(BF)
-        dk = dot(ds, qs[...], NN) * SCALE
-        dqT[...] += dot(kv[zs, 0, rows, :].T, ds, NN)
-        return dk, dv
+        dk = dv = None
+        for side in range(2):
+            cols = slice(side * TOK, (side + 1) * TOK)
+            factor = jnp.exp2((mst[zs, half, :, cols] - mrow[:, cols]) * EXP2_SCALE) / lrow[:, cols]
+            dob = (dof[:, cols] * factor).astype(BF)
+            delta = jnp.sum(dob.astype(F32) * aT[:, cols], axis=0, keepdims=True)
+            p = pst[zs, half, :, cols]
+            dv_side = dot(p, dob, NT)
+            dp = dot(kv[zs, 1, rows, :], dob, NN)
+            ds = (p.astype(F32) * (dp - delta)).astype(BF)
+            pst[zs, half, :, cols] = ds
+            dk_side = dot(ds, qs[cols, :], NN)
+            dk = dk_side if side == 0 else dk + dk_side
+            dv = dv_side if side == 0 else dv + dv_side
+        return dk * SCALE, dv
+
+    def query_step(zs, carry):
+        both = dot(kv[zs, 0, :HALF, :].T, pst[zs, 0], NN)
+        dqT[...] += both + dot(kv[zs, 0, HALF:, :].T, pst[zs, 1], NN)
+        return carry
 
     own_attn = afull.at[xc, q_rows, :]
 
@@ -422,22 +421,30 @@
 
         @pl.when(u == 0)
         def _():
+            osend[...] = aT[...].T.astype(BF)
+            for k in range(NX):
+                far, near = o_copies(k)
+                if k:
+                    far.start()
+                else:
+                    pl.when(c != xc)(far.start)
+                    pl.when(c == xc)(near.start)
             sb_wait(0)
             for a in range(2):
                 ring(a, 4, a)
 
         @pl.when(u == 1)
         def _():
+            sb_wait(1)
+            ring(0, 3, 1)
+
+        @pl.when(u == 2)
+        def _():
+            sb_wait(2)
+            ring(1, 3, 0)
             for k in range(1, NX):
                 await_at(gx.at[xplus(-k), c], gx_recv.at[k])
                 gx_forward(k).start()
-
-        @pl.when(u == 2)
-        def _():
-            sb_wait(1)
-            sb_wait(2)
-            for direction in range(2):
-                ring(direction, 3, 1 - direction)
 
         @pl.when(u == 3)
         def _():
@@ -481,14 +488,16 @@
 
     lax.fori_loop(0, 8, backward_step, 0)
 
-    gsend[2] = (dqT[...] * SCALE).T.astype(BF)
-    for r in range(2):
-        start_either(*f_copies(r, 2), r)
+    lax.fori_loop(0, 4, query_step, 0)
     sb_wait(5)
     sb_wait(6)
     for direction in range(2):
         ring(direction, 1, 1 - direction)
     wz_middle()
+    lax.fori_loop(4, 8, query_step, 0)
+    gsend[2] = (dqT[...] * SCALE).T.astype(BF)
+    for r in range(2):
+        start_either(*f_copies(r, 2), r)
     for direction in range(2):
         ring(direction, 1, direction)
     for k in (1, 2, 3):
@@ -503,7 +512,9 @@
     o = jnp.zeros((TOK, TOK), F32)
     for h in range(8):
         o = o + dot(aall[h], w_all[h], NN)
-    out_ref[...] = o.astype(BF)
+    out_vm[...] = o.astype(BF)
+    out_store = pltpu.make_async_copy(out_vm, out_ref, l_sem.at[2])
+    out_store.start()
 
     for e in range(2):
         for a in range(3):
@@ -536,37 +547,42 @@
             left(kv.at[0, :, pl.ds(0, HALF), :], ag_send.at[direction, dist - 1])
         left(kv.at[0, 0, pl.ds(0, HALF), :], ag_send.at[direction, 3])
 
-    for e in range(2):
-        await_at(gq.at[e], f_recv.at[e, 2])
-        dq_ref[:, e * HD:(e + 1) * HD] = gq[e]
-    for e in range(2):
-        for a in range(2):
-            await_at(gkv.at[2, e, a], f_recv.at[e, a])
-
     wg = wgp[z]
     for kind in (2, 3):
         for direction in range(2):
             wz_wait(kind, direction)
             wg = wg + wz_in[kind, direction].astype(F32)
-    wg_ref[...] = wg.astype(BF)
+    wg_vm[...] = wg.astype(BF)
+    wg_store = pltpu.make_async_copy(wg_vm, wg_ref, l_sem.at[3])
+    wg_store.start()
     left(wz_out.at[0, 0], wz_send.at[0])
     left(wz_out.at[pl.ds(0, 3)], wz_send.at[1])
 
-    for a, ref in ((1, dv_ref), (0, dk_ref)):
-        for e in range(2):
-            for direction in range(2):
-                await_at(gkv.at[direction, e, a], g_recv.at[direction, e, a])
-            value = gkv[0, e, a].astype(F32) + gkv[1, e, a].astype(F32) + gkv[2, e, a].astype(F32)
-            ref[:, e * HD:(e + 1) * HD] = value.astype(BF)
+    for e in range(2):
+        await_at(gq.at[e], f_recv.at[e, 2])
+        for a in range(2):
+            await_at(gkv.at[2, e, a], f_recv.at[e, a])
+    out_store.wait()
+    wg_store.wait()
     for direction in range(2):
         for r in range(2):
             for a in range(2):
                 g_copy(direction, r, a).wait_send()
-
-
-def copy_kernel(*refs):
-    for n in range(5):
-        refs[5 + n][...] = refs[n][...]
+    for a in range(2):
+        for e in range(2):
+            for direction in range(2):
+                await_at(gkv.at[direction, e, a], g_recv.at[direction, e, a])
+
+
+def last_kernel(held_out, gq, gkv, held_wg, out_ref, dq_ref, dk_ref, dv_ref, wg_ref):
+    out_ref[...] = held_out[...]
+    wg_ref[...] = held_wg[...]
+    for e in range(2):
+        cols = slice(e * HD, (e + 1) * HD)
+        dq_ref[:, cols] = gq[e]
+        for a, ref in ((0, dk_ref), (1, dv_ref)):
+            value = gkv[0, e, a].astype(F32) + gkv[1, e, a].astype(F32) + gkv[2, e, a].astype(F32)
+            ref[:, cols] = value.astype(BF)
 
 
 def on_device(queries, key_rows, value_rows, w_out, out_grad, tile_kind):
@@ -604,9 +620,9 @@
         V((4, 2, 64, TOK), BF),
         V((4, 2, 64, TOK), BF),
         V((3, HALF, HD), BF),
-        V((2, TOK, HD), BF),
-        V((3, 2, 2, TOK, HD), BF),
-        S(2), S(2, 3), S(2, 3), S(2, 4), S(2, 4, 2, 2), S(1), S(8, 2),
+        V((TOK, TOK), BF),
+        V((64, TOK), BF),
+        S(4), S(2, 3), S(2, 3), S(2, 4), S(2, 4, 2, 2), S(1), S(8, 2),
         S(1), S(4), S(1), S(4), S(1), S(8), S(2), S(2),
         S(1), S(4), S(1), S(4),
         S(4), S(2, 2), S(1), S(4), S(1), S(4),
@@ -617,9 +633,9 @@
     outs = [shape(TOK, TOK)] * 4 + [shape(64, TOK)]
     held = pl.pallas_call(
         kernel,
-        out_shape=outs,
+        out_shape=[shape(TOK, TOK), shape(2, TOK, HD), shape(3, 2, 2, TOK, HD), shape(64, TOK)],
         in_specs=[anywhere] * 5 + [smem],
-        out_specs=[vmem] * 5,
+        out_specs=[anywhere] * 4,
         scratch_shapes=scratch,
         compiler_params=pltpu.CompilerParams(
             collective_id=0, has_side_effects=True, vmem_limit_bytes=56 * 1024 * 1024
@@ -627,7 +643,7 @@
         cost_estimate=pl.CostEstimate(flops=8 * 10**9, bytes_accessed=4 * 10**6, transcendentals=0),
     )(queries, key_rows, value_rows, w_out, out_grad, tile_kind)
     out, dq, dk, dv, wg = pl.pallas_call(
-        copy_kernel, out_shape=outs, in_specs=[vmem] * 5, out_specs=[vmem] * 5
+        last_kernel, out_shape=outs, in_specs=[vmem] * 4, out_specs=[vmem] * 5
     )(*held)
     return out, dq, dk, dv, wg.T
 

time: 74.1 us -> 72.9 us (0.984)
  Pallas kernels: 73.2 us -> 72 us
    pallas_call x2, Pallas kernels: 73.2 us -> 72 us  [the longest x1 69.9 us: on_device(): pl.pallas_call(kernel, out_shape=[shape(TOK, TOK), shape(2, TOK, HD), sha...]
where the time goes in v4:
time: 72.9 us; the launch traced here: 72.6 us
  Pallas kernels  72 us (99%)
    pallas_call x1, Pallas kernels, on_device(): pl.pallas_call(kernel, out_shape=[shape(TOK, TOK), shape(2, TOK, HD), sha...  69.9 us
    pallas_call x1, Pallas kernels, on_device(): pl.pallas_call(last_kernel, out_shape=outs, in_specs=[vmem] * 4, out_spec...  2.11 us

profile of v4, /device:TPU:1, one launch (start us, length us, event | category | flops | bytes accessed | tf_op | source)
XLA Modules:
  0.0 72.6 jit_solution(14241063829585353443)
XLA Ops:
  0.6 69.9 %shard_map.101 = (bf16[256,256]{1,0:T(8,128)(2,1)}, bf16[2,256,128]{2,1,0:T(8,128)(2,1)}, bf16[3,2,2,256,128]{4,3,2,1,0:T(8,128)(2,1)}, bf16[64,256]{1,0:T(8,128)(2,1)}) custom-call(bf16[256,256]{1,0:T(8,128)(2,1)} %q_ref.1, bf16[256,256]{1,0:T(8,128)(2,1)} %k_ref.1, bf16[256,256]{1,0:T(8,128)(2,1)} %v_ref.1, bf16[256,2048]{1,0:T(8,128)(2,1)} %w_ref.1, ...), custom_call_target="tpu_custom_call" | custom-call | flops 8000000000 | bytes 4000000 | tf_op jit(solution)/shard_map/pallas_call | solution.py:634
  70.5 2.1 %shard_map.102 = (bf16[256,256]{1,0:T(8,128)(2,1)}, bf16[256,256]{1,0:T(8,128)(2,1)}, bf16[256,256]{1,0:T(8,128)(2,1)}, bf16[256,256]{1,0:T(8,128)(2,1)}, bf16[64,256]{1,0:T(8,128)(2,1)}) custom-call(bf16[256,256]{1,0:T(8,128)(2,1)} %get-tuple-element.14.held_out, bf16[2,256,128]{2,1,0:T(8,128)(2,1)} %get-tuple-element.15.gq, ...), custom_call_target="tpu_custom_call" | custom-call | tf_op jit(solution)/shard_map/pallas_call | solution.py:645

commit v5 on v4

--- a/solution.py
+++ b/solution.py
@@ -30,7 +30,7 @@
 def kernel(
     q_ref, k_ref, v_ref, w_ref, g_ref, kind_ref,
     out_ref, gq, gkv, wg_ref,
-    kv, qs, dos, pst, mst, oT, dqT, mrow, lrow, aT, dof,
+    kv, qs, dos, pst, mst, oT, dqT, mrow, lrow, aT, dof, delta,
     w_in, g_all, w_all, dsend, gx, osend, afull, aall,
     part, sib_out, sib_in, rs_out, rs_in, wgp, wz_out, wz_in, gsend, out_vm, wg_vm,
     l_sem, a_send, a_recv, ag_send, ag_recv, sib_send, sib_recv,
@@ -202,10 +202,12 @@
         ref = gx.at[xplus(-k), c]
         return remote(ref, ref, gxf_send.at[0], gxf_recv.at[k], sibling)
 
+    def chunk_of(t):
+        return zplus(lax.div(t + 1, 2) * (1 - 2 * lax.rem(t, 2)))
+
     def forward_step(t, carry):
         dist = lax.div(t + 1, 2)
-        odd = lax.rem(t, 2)
-        zs = zplus(dist * (1 - 2 * odd))
+        zs = chunk_of(t)
 
         def arrival(e, dist):
             a, h = lax.rem(e, 2), lax.div(e, 2)
@@ -281,17 +283,18 @@
                 gx[x, h] = g_all[2 * x + h]
             w_all[j] = w_in[:, pl.ds(pl.multiple_of(j * TOK, TOK), TOK)]
 
-        @pl.when(t == 6)
-        def _():
-            for r in range(2):
-                await_at(dos.at[pl.ds(r * TOK, TOK), :], d_recv.at[r])
-            dof[...] = dos[...].astype(F32).T
-
         forward_unit(zs, c)
         slot(2 * t + 1)
         for r in range(2):
             await_at(pair(zs, 1 - c, r), sib_recv.at[t, r])
         forward_unit(zs, 1 - c)
+
+        @pl.when(t == 6)
+        def _():
+            for r in range(2):
+                await_at(dos.at[pl.ds(r * TOK, TOK), :], d_recv.at[r])
+            dof[...] = dos[...].astype(F32).T
+
         return carry
 
     lax.fori_loop(0, 8, forward_step, 0)
@@ -299,6 +302,7 @@
     inv = 1.0 / lrow[...]
     attnT = (oT[...] * inv).astype(BF).astype(F32)
     aT[...] = attnT
+    delta[...] = jnp.sum(dof[...] * attnT, axis=0, keepdims=True)
 
     def o_copies(k):
         dst = afull.at[c, :, pl.ds(pl.multiple_of(xr * HD, HD), HD)]
@@ -380,12 +384,10 @@
         for side in range(2):
             cols = slice(side * TOK, (side + 1) * TOK)
             factor = jnp.exp2((mst[zs, half, :, cols] - mrow[:, cols]) * EXP2_SCALE) / lrow[:, cols]
-            dob = (dof[:, cols] * factor).astype(BF)
-            delta = jnp.sum(dob.astype(F32) * aT[:, cols], axis=0, keepdims=True)
-            p = pst[zs, half, :, cols]
-            dv_side = dot(p, dob, NT)
-            dp = dot(kv[zs, 1, rows, :], dob, NN)
-            ds = (p.astype(F32) * (dp - delta)).astype(BF)
+            p = pst[zs, half, :, cols].astype(F32) * factor
+            dp = dot(kv[zs, 1, rows, :], dos[cols, :], NT)
+            ds = (p * (dp - delta[:, cols])).astype(BF)
+            dv_side = dot(p.astype(BF), dos[cols, :], NN)
             pst[zs, half, :, cols] = ds
             dk_side = dot(ds, qs[cols, :], NN)
             dk = dk_side if side == 0 else dk + dk_side
@@ -603,6 +605,7 @@
         V((1, HALF), F32),
         V((HD, HALF), F32),
         V((HD, HALF), F32),
+        V((1, HALF), F32),
         V((TOK, 8 * TOK), BF),
         V((8, TOK, TOK), BF),
         V((8, TOK, TOK), BF),

time: 72.9 us -> 72.1 us (0.989)
  Pallas kernels: 72 us -> 71.2 us
    pallas_call x1, Pallas kernels: 69.9 us -> 69.1 us  [on_device(): pl.pallas_call(kernel, out_shape=[shape(TOK, TOK), shape(2, TOK, HD), sha...]
where the time goes in v5:
time: 72.1 us; the launch traced here: 71.8 us
  Pallas kernels  71.2 us (99%)
    pallas_call x1, Pallas kernels, on_device(): pl.pallas_call(kernel, out_shape=[shape(TOK, TOK), shape(2, TOK, HD), sha...  69.1 us
    pallas_call x1, Pallas kernels, on_device(): pl.pallas_call(last_kernel, out_shape=outs, in_specs=[vmem] * 4, out_spec...  2.11 us

profile of v5, /device:TPU:1, one launch (start us, length us, event | category | flops | bytes accessed | tf_op | source)
XLA Modules:
  0.0 71.8 jit_solution(10185636756102961986)
XLA Ops:
  0.6 69.1 %shard_map.101 = (bf16[256,256]{1,0:T(8,128)(2,1)}, bf16[2,256,128]{2,1,0:T(8,128)(2,1)}, bf16[3,2,2,256,128]{4,3,2,1,0:T(8,128)(2,1)}, bf16[64,256]{1,0:T(8,128)(2,1)}) custom-call(bf16[256,256]{1,0:T(8,128)(2,1)} %q_ref.1, bf16[256,256]{1,0:T(8,128)(2,1)} %k_ref.1, bf16[256,256]{1,0:T(8,128)(2,1)} %v_ref.1, bf16[256,2048]{1,0:T(8,128)(2,1)} %w_ref.1, ...), custom_call_target="tpu_custom_call" | custom-call | flops 8000000000 | bytes 4000000 | tf_op jit(solution)/shard_map/pallas_call | solution.py:637
  69.7 2.1 %shard_map.102 = (bf16[256,256]{1,0:T(8,128)(2,1)}, bf16[256,256]{1,0:T(8,128)(2,1)}, bf16[256,256]{1,0:T(8,128)(2,1)}, bf16[256,256]{1,0:T(8,128)(2,1)}, bf16[64,256]{1,0:T(8,128)(2,1)}) custom-call(bf16[256,256]{1,0:T(8,128)(2,1)} %get-tuple-element.14.held_out, bf16[2,256,128]{2,1,0:T(8,128)(2,1)} %get-tuple-element.15.gq, ...), custom_call_target="tpu_custom_call" | custom-call | tf_op jit(solution)/shard_map/pallas_call | solution.py:648

commit v6 on v5

--- a/solution.py
+++ b/solution.py
@@ -147,6 +147,10 @@
         ref = pair(zs, c, r)
         return remote(ref, ref, sib_send.at[0], sib_recv.at[t, r], sibling)
 
+    def last_sib_copy(a, zs):
+        ref = kv.at[zs, a, half_rows, :]
+        return remote(ref, ref, sib_send.at[0], sib_recv.at[7, a], sibling)
+
     kpos = lax.broadcasted_iota(jnp.int32, (TILE, HALF), 0)
     qpos = lax.broadcasted_iota(jnp.int32, (TILE, HALF), 1) % TILE
     diff = kpos - qpos
@@ -154,7 +158,7 @@
     def block_of(half, b, zs):
         return 2 * ((2 * half + b // 2) * NZ + zs) + b % 2
 
-    def forward_unit(zs, half):
+    def forward_unit(zs, half, values_wait):
         rows = pl.ds(pl.multiple_of(half * HALF, HALF), HALF)
         s = dot(kv[zs, 0, rows, :], qs[...], NT)
         parts = []
@@ -174,9 +178,9 @@
         lrow[...] = lrow[...] * alpha + jnp.sum(p, axis=0, keepdims=True)
         mrow[...] = new
         mst[zs, half] = new
-        pb = p.astype(BF)
-        pst[zs, half] = pb
-        oT[...] = oT[...] * alpha + dot(kv[zs, 1, rows, :].T, pb, NN)
+        pst[zs, half] = p.astype(BF)
+        values_wait()
+        oT[...] = oT[...] * alpha + dot(kv[zs, 1, rows, :].T, pst[zs, half], NN)
 
     mrow[...] = jnp.full(mrow.shape, NEG, F32)
     lrow[...] = jnp.zeros(lrow.shape, F32)
@@ -247,9 +251,8 @@
         @pl.when(t == 7)
         def _():
             for r in range(2):
-                for a in range(2):
-                    await_at(piece(zs, a, r), ag_recv.at[r, 3, a, r])
-                sib_copy(t, r, zs).start()
+                await_at(piece(zs, 0, r), ag_recv.at[r, 3, 0, r])
+            last_sib_copy(0, zs).start()
 
         slot(2 * t)
 
@@ -283,11 +286,33 @@
                 gx[x, h] = g_all[2 * x + h]
             w_all[j] = w_in[:, pl.ds(pl.multiple_of(j * TOK, TOK), TOK)]
 
-        forward_unit(zs, c)
+        other_rows = pl.ds(pl.multiple_of((1 - c) * HALF, HALF), HALF)
+
+        def values_here():
+            @pl.when(t == 7)
+            def _():
+                for r in range(2):
+                    await_at(piece(zs, 1, r), ag_recv.at[r, 3, 1, r])
+                last_sib_copy(1, zs).start()
+
+        def values_there():
+            @pl.when(t == 7)
+            def _():
+                await_at(kv.at[zs, 1, other_rows, :], sib_recv.at[7, 1])
+
+        forward_unit(zs, c, values_here)
         slot(2 * t + 1)
-        for r in range(2):
-            await_at(pair(zs, 1 - c, r), sib_recv.at[t, r])
-        forward_unit(zs, 1 - c)
+
+        @pl.when(t < 7)
+        def _():
+            for r in range(2):
+                await_at(pair(zs, 1 - c, r), sib_recv.at[t, r])
+
+        @pl.when(t == 7)
+        def _():
+            await_at(kv.at[zs, 0, other_rows, :], sib_recv.at[7, 0])
+
+        forward_unit(zs, 1 - c, values_there)
 
         @pl.when(t == 6)
         def _():

time: 72.1 us -> 72.1 us (level)
  no operation moved by 1% of the time
where the time goes in v6:
time: 72.1 us; the launch traced here: 71.8 us
  Pallas kernels  71.2 us (99%)
    pallas_call x1, Pallas kernels, on_device(): pl.pallas_call(kernel, out_shape=[shape(TOK, TOK), shape(2, TOK, HD), sha...  69.1 us
    pallas_call x1, Pallas kernels, on_device(): pl.pallas_call(last_kernel, out_shape=outs, in_specs=[vmem] * 4, out_spec...  2.11 us

profile of v6, /device:TPU:1, one launch (start us, length us, event | category | flops | bytes accessed | tf_op | source)
XLA Modules:
  0.0 71.8 jit_solution(12261737698501525979)
XLA Ops:
  0.6 69.1 %shard_map.101 = (bf16[256,256]{1,0:T(8,128)(2,1)}, bf16[2,256,128]{2,1,0:T(8,128)(2,1)}, bf16[3,2,2,256,128]{4,3,2,1,0:T(8,128)(2,1)}, bf16[64,256]{1,0:T(8,128)(2,1)}) custom-call(bf16[256,256]{1,0:T(8,128)(2,1)} %q_ref.1, bf16[256,256]{1,0:T(8,128)(2,1)} %k_ref.1, bf16[256,256]{1,0:T(8,128)(2,1)} %v_ref.1, bf16[256,2048]{1,0:T(8,128)(2,1)} %w_ref.1, ...), custom_call_target="tpu_custom_call" | custom-call | flops 8000000000 | bytes 4000000 | tf_op jit(solution)/shard_map/pallas_call | solution.py:662
  69.7 2.1 %shard_map.102 = (bf16[256,256]{1,0:T(8,128)(2,1)}, bf16[256,256]{1,0:T(8,128)(2,1)}, bf16[256,256]{1,0:T(8,128)(2,1)}, bf16[256,256]{1,0:T(8,128)(2,1)}, bf16[64,256]{1,0:T(8,128)(2,1)}) custom-call(bf16[256,256]{1,0:T(8,128)(2,1)} %get-tuple-element.14.held_out, bf16[2,256,128]{2,1,0:T(8,128)(2,1)} %get-tuple-element.15.gq, ...), custom_call_target="tpu_custom_call" | custom-call | tf_op jit(solution)/shard_map/pallas_call | solution.py:673
